TPU v7x, 128 devices: a whole 4x4x4 slice. The times are simulated.
128 devices in a mesh: img: 8 (over z, y_hi), txt: 16 (over y_lo, x, core).
Axes of the slice: x: 4, y: 4 (y_hi: 2, y_lo: 2; y = y_hi * 2 + y_lo), z: 4, core: 2. Of those that a mesh axis runs over, the one named last changes fastest.
Arguments:
- image_emb: bfloat16 [16384, 1152], P(('img', 'txt')), may hold values from -0.19921875 to 0.19921875
- text_emb: bfloat16 [16384, 1152], P(('txt', 'img')), may hold values from -0.19921875 to 0.19921875
- positive: int32 [16384], P('img'), may hold values from 0 to 16383, each once
- log_scale: float32 [], replicated, may hold values from 1.5 to 2.5
- bias: float32 [], replicated, may hold values from -10 to -6
Outputs:
- loss: float32 [], replicated
- image_grad: float32 [16384, 1152], P(('img', 'txt'))
- text_grad: float32 [16384, 1152], P(('txt', 'img'))
- scale_grad: float32 [], replicated
- bias_grad: float32 [], replicated
Inputs may be any that keep to these rules, and one draw needn't show every extreme that they name: Each text row is the positive of exactly one image row.
All inputs are finite; a program needn't handle non-finite values.
Results may differ from a plain program's by a relative error of at most 0.0042.
Values may be sent and summed in bfloat16 or wider, within the bound.
A program may use at most 128 MiB of HBM per device.

v0:
```python
import math

import jax
import jax.numpy as jnp
from jax import lax
from jax.sharding import PartitionSpec as P

EPS = 1e-06


def unit_rows(emb):
    values = emb.astype(jnp.float32)
    norm = jnp.sqrt(jnp.sum(values * values, axis=1, keepdims=True) + EPS)
    return (values / norm, norm)


def project_rows(summed, unit, norm):
    return (summed - unit * jnp.sum(unit * summed, axis=1, keepdims=True)) / norm


def body(image_emb, text_emb, positive, log_scale, bias):
    image_full = lax.all_gather(image_emb, "txt", axis=0, tiled=True)
    text_full = lax.all_gather(text_emb, "img", axis=0, tiled=True)
    image_unit, image_norm = unit_rows(image_full)
    text_unit, text_norm = unit_rows(text_full)
    image_low = image_unit.astype(jnp.bfloat16)
    text_low = text_unit.astype(jnp.bfloat16)
    scale = jnp.exp(log_scale)
    image_rows, width = image_full.shape
    text_rows = text_full.shape[0]
    columns = lax.axis_index("txt") * text_rows + jnp.arange(text_rows, dtype=jnp.int32)
    block = math.gcd(image_rows, 512)
    count = image_rows // block

    def step(carry, inputs):
        text_acc, loss_acc, weight_acc, cos_acc = carry
        rows_low, rows_pos = inputs
        cosine = lax.dot_general(
            rows_low, text_low, (((1,), (1,)), ((), ())), preferred_element_type=jnp.float32
        )
        logit = scale * cosine + bias
        sign = jnp.where(rows_pos[:, None] == columns[None, :], 1.0, -1.0).astype(jnp.float32)
        margin = -sign * logit
        weight = -sign * jax.nn.sigmoid(margin)
        weight_low = weight.astype(jnp.bfloat16)
        image_part = jnp.dot(weight_low, text_low, preferred_element_type=jnp.float32)
        text_acc = text_acc + lax.dot_general(
            weight_low, rows_low, (((0,), (0,)), ((), ())), preferred_element_type=jnp.float32
        )
        carry = (
            text_acc,
            loss_acc + jnp.sum(jax.nn.softplus(margin)),
            weight_acc + jnp.sum(weight),
            cos_acc + jnp.sum(weight * cosine),
        )
        return (carry, image_part)

    start = (
        jnp.zeros((text_rows, width), jnp.float32),
        jnp.zeros((), jnp.float32),
        jnp.zeros((), jnp.float32),
        jnp.zeros((), jnp.float32),
    )
    inputs = (image_low.reshape(count, block, width), positive.reshape(count, block))
    (text_acc, loss_part, weight_part, cos_part), image_parts = lax.scan(step, start, inputs)
    image_partial = scale * image_parts.reshape(image_rows, width)
    text_partial = scale * text_acc
    image_own = image_emb.shape[0]
    text_own = text_emb.shape[0]
    image_start = lax.axis_index("txt") * image_own
    text_start = lax.axis_index("img") * text_own
    image_hat = lax.dynamic_slice_in_dim(image_unit, image_start, image_own, 0)
    image_scale = lax.dynamic_slice_in_dim(image_norm, image_start, image_own, 0)
    text_hat = lax.dynamic_slice_in_dim(text_unit, text_start, text_own, 0)
    text_scale = lax.dynamic_slice_in_dim(text_norm, text_start, text_own, 0)
    image_piece = lax.psum_scatter(image_partial, "txt", scatter_dimension=0, tiled=True)
    text_piece = lax.psum_scatter(text_partial, "img", scatter_dimension=0, tiled=True)
    image_grad = project_rows(image_piece, image_hat, image_scale)
    text_grad = project_rows(text_piece, text_hat, text_scale)
    loss_sum, weight_sum, cos_sum = lax.psum((loss_part, weight_part, cos_part), ("img", "txt"))
    pairs = image_rows * lax.axis_size("img")
    return (loss_sum / pairs, image_grad, text_grad, scale * cos_sum, weight_sum)


def solution(mesh):
    placed = (P(("img", "txt"), None), P(("txt", "img"), None), P("img"), P(), P())
    return jax.shard_map(
        body,
        mesh=mesh,
        in_specs=placed,
        out_specs=(P(), P(("img", "txt"), None), P(("txt", "img"), None), P(), P()),
        check_vma=False,
    )
```

profile of v0, /device:TPU:0, one launch (start us, length us, event | category | flops | bytes accessed | tf_op | source)
XLA Modules:
  0.0 387.4 jit_solution(17691318441123830839)
XLA Ops:
  7.2 0.0 all-gather.5.cloned.1.call-start
  7.2 0.7 all-gather.5.cloned.1.call-update
  7.9 0.0 all-gather.3.cloned.1.call-start
  7.9 0.7 all-gather.3.cloned.1.call-update
  8.6 0.0 reduce-scatter.5.cloned.1.call-start
  9.4 0.7 reshape.58
  10.1 59.1 %all-gather.5.cloned.1.call-done = bf16[1024,1152]{1,0:T(8,128)(2,1)} async-done(((bf16[128,1152]{1,0:T(8,128)(2,1)}), bf16[1024,1152]{1,0:T(8,128)(2,1)}) %all-gather.5.cloned.1.call-update) | async-done | bytes 2359312 | tf_op jit(solution)/shard_map/all_gather | solution.py:23
  69.2 0.0 copy-start.1
  69.2 2.3 fusion.15
  71.6 0.0 copy-done.1
  71.6 2.9 convert_divide_fusion.1
  74.5 32.6 %all-gather.3.cloned.1.call-done = bf16[2048,1152]{1,0:T(8,128)(2,1)} async-done(((bf16[128,1152]{1,0:T(8,128)(2,1)}), bf16[2048,1152]{1,0:T(8,128)(2,1)}) %all-gather.3.cloned.1.call-update) | async-done | bytes 4718608 | tf_op jit(solution)/shard_map/all_gather | solution.py:22
  107.1 0.0 copy-start
  107.1 3.5 fusion.14
  110.5 0.3 copy-done
  110.8 6.7 %convert_divide_fusion = (f32[2048,1152]{1,0:T(8,128)}, bf16[2048,1152]{1,0:T(8,128)(2,1)}) fusion(bf16[2048,1152]{1,0:T(8,128)(2,1)S(1)} %copy-done, f32[2048]{0:T(1024)S(1)} %add_sqrt_fusion), kind=kLoop, calls=%fused_computation.22 | loop fusion | flops 7077888 | bytes 18882560 | tf_op jit(solution)/shard_map/div | solution.py:14
  117.6 85.7 %while.19 = (s32[]{:T(128)}, f32[1024,1152]{1,0:T(8,128)}, f32[]{:T(128)}, f32[]{:T(128)}, f32[]{:T(128)}, /*index=5*/f32[4,512,1152]{2,1,0:T(8,128)}, s32[4,512...) while((s32[]{:T(128)}, f32[1024,1152]{1,0:T(8,128)}, ...), condition=%wide.region_6.7_spmd.clone, body=%wide.region_2.6_spmd.clone.sunk | while | flops 3648259072 | bytes 33584376 | solution.py:65
  117.6 7.2 %multiply_reduce_fusion.4 = (f32[]{:T(128)}, f32[]{:T(128)}, f32[]{:T(128)}, f32[512,1024]{1,0:T(8,128)}) fusion(f32[]{:T(128)} %get-tuple-element.272, f32[]{:T(128)} %get-tuple-element.269, s32[1024]{0:T(1024)S(1)} %iota_add_fusion.2, s32[512]{0:T(512)S(1)} %bitcast.30, bf16[1024,1152]{1,0:T(8,128)(2,1)S(1)} %get-tuple-element.271, ...), kind=kOutput, calls=%fused_computation.6.clone.1 | convolution fusion | flops 1218445312 | bytes 5643280 | tf_op jit(solution)/shard_map/while/body/eval_jaxpr/dot_general | solution.py:38
  126.8 0.0 copy-start.2
  126.8 6.9 %convolution_add_fusion.2 = f32[1024,1152]{1,0:T(8,128)} fusion(f32[1024,1152]{1,0:T(8,128)} %get-tuple-element.249, pred[]{:T(512)S(6)} %compare.3, bf16[4,512,1152]{2,1,0:T(8,128)(2,1)} %get-tuple-element.270, s32[]{:T(128)S(6)} %copy.17, f32[512,1024]{1,0:T(8,128)} %get-tuple-element.230, f32[]{:T(128)} %get-tuple-element.272, ...), kind=kOutput, calls=%fused_computation.2.clone.1 | convolution fusion | flops 1216086016 | bytes 12721157 | tf_op jit(solution)/shard_map/while/body/eval_jaxpr/dot_general | solution.py:47
  133.7 0.0 copy-done.2
  133.7 4.2 %fusion.31 = f32[4,512,1152]{2,1,0:T(8,128)} fusion(f32[4,512,1152]{2,1,0:T(8,128)} %get-tuple-element.253, s32[]{:T(128)S(6)} %copy.17, bf16[1024,1152]{1,0:T(8,128)(2,1)S(1)} %get-tuple-element.271, f32[512,1024]{1,0:T(8,128)S(1)} %copy-done.2, f32[]{:T(128)} %get-tuple-element.272, f32[]{:T(128)} %get-tuple-element.269, ...), kind=kOutput, calls=%fused_computation.4.clone.1 | convolution fusion | flops 1213726720 | bytes 6822916 | tf_op jit(solution)/shard_map/while/body/eval_jaxpr/dot_general | solution.py:46
  137.9 7.2 %multiply_reduce_fusion.4 = (f32[]{:T(128)}, f32[]{:T(128)}, f32[]{:T(128)}, f32[512,1024]{1,0:T(8,128)}) fusion(f32[]{:T(128)} %get-tuple-element.272, f32[]{:T(128)} %get-tuple-element.269, s32[1024]{0:T(1024)S(1)} %iota_add_fusion.2, s32[512]{0:T(512)S(1)} %bitcast.30, bf16[1024,1152]{1,0:T(8,128)(2,1)S(1)} %get-tuple-element.271, ...), kind=kOutput, calls=%fused_computation.6.clone.1 | convolution fusion | flops 1218445312 | bytes 5643280 | tf_op jit(solution)/shard_map/while/body/eval_jaxpr/dot_general | solution.py:38
  147.1 0.0 copy-start.2
  147.1 8.4 %convolution_add_fusion.2 = f32[1024,1152]{1,0:T(8,128)} fusion(f32[1024,1152]{1,0:T(8,128)} %get-tuple-element.249, pred[]{:T(512)S(6)} %compare.3, bf16[4,512,1152]{2,1,0:T(8,128)(2,1)} %get-tuple-element.270, s32[]{:T(128)S(6)} %copy.17, f32[512,1024]{1,0:T(8,128)} %get-tuple-element.230, f32[]{:T(128)} %get-tuple-element.272, ...), kind=kOutput, calls=%fused_computation.2.clone.1 | convolution fusion | flops 1216086016 | bytes 12721157 | tf_op jit(solution)/shard_map/while/body/eval_jaxpr/dot_general | solution.py:47
  155.5 0.0 copy-done.2
  155.5 4.3 %fusion.31 = f32[4,512,1152]{2,1,0:T(8,128)} fusion(f32[4,512,1152]{2,1,0:T(8,128)} %get-tuple-element.253, s32[]{:T(128)S(6)} %copy.17, bf16[1024,1152]{1,0:T(8,128)(2,1)S(1)} %get-tuple-element.271, f32[512,1024]{1,0:T(8,128)S(1)} %copy-done.2, f32[]{:T(128)} %get-tuple-element.272, f32[]{:T(128)} %get-tuple-element.269, ...), kind=kOutput, calls=%fused_computation.4.clone.1 | convolution fusion | flops 1213726720 | bytes 6822916 | tf_op jit(solution)/shard_map/while/body/eval_jaxpr/dot_general | solution.py:46
  159.8 7.2 %multiply_reduce_fusion.4 = (f32[]{:T(128)}, f32[]{:T(128)}, f32[]{:T(128)}, f32[512,1024]{1,0:T(8,128)}) fusion(f32[]{:T(128)} %get-tuple-element.272, f32[]{:T(128)} %get-tuple-element.269, s32[1024]{0:T(1024)S(1)} %iota_add_fusion.2, s32[512]{0:T(512)S(1)} %bitcast.30, bf16[1024,1152]{1,0:T(8,128)(2,1)S(1)} %get-tuple-element.271, ...), kind=kOutput, calls=%fused_computation.6.clone.1 | convolution fusion | flops 1218445312 | bytes 5643280 | tf_op jit(solution)/shard_map/while/body/eval_jaxpr/dot_general | solution.py:38
  169.0 0.0 copy-start.2
  169.0 8.4 %convolution_add_fusion.2 = f32[1024,1152]{1,0:T(8,128)} fusion(f32[1024,1152]{1,0:T(8,128)} %get-tuple-element.249, pred[]{:T(512)S(6)} %compare.3, bf16[4,512,1152]{2,1,0:T(8,128)(2,1)} %get-tuple-element.270, s32[]{:T(128)S(6)} %copy.17, f32[512,1024]{1,0:T(8,128)} %get-tuple-element.230, f32[]{:T(128)} %get-tuple-element.272, ...), kind=kOutput, calls=%fused_computation.2.clone.1 | convolution fusion | flops 1216086016 | bytes 12721157 | tf_op jit(solution)/shard_map/while/body/eval_jaxpr/dot_general | solution.py:47
  177.3 0.0 copy-done.2
  177.3 4.2 %fusion.31 = f32[4,512,1152]{2,1,0:T(8,128)} fusion(f32[4,512,1152]{2,1,0:T(8,128)} %get-tuple-element.253, s32[]{:T(128)S(6)} %copy.17, bf16[1024,1152]{1,0:T(8,128)(2,1)S(1)} %get-tuple-element.271, f32[512,1024]{1,0:T(8,128)S(1)} %copy-done.2, f32[]{:T(128)} %get-tuple-element.272, f32[]{:T(128)} %get-tuple-element.269, ...), kind=kOutput, calls=%fused_computation.4.clone.1 | convolution fusion | flops 1213726720 | bytes 6822916 | tf_op jit(solution)/shard_map/while/body/eval_jaxpr/dot_general | solution.py:46
  181.5 7.2 %multiply_reduce_fusion.4 = (f32[]{:T(128)}, f32[]{:T(128)}, f32[]{:T(128)}, f32[512,1024]{1,0:T(8,128)}) fusion(f32[]{:T(128)} %get-tuple-element.272, f32[]{:T(128)} %get-tuple-element.269, s32[1024]{0:T(1024)S(1)} %iota_add_fusion.2, s32[512]{0:T(512)S(1)} %bitcast.30, bf16[1024,1152]{1,0:T(8,128)(2,1)S(1)} %get-tuple-element.271, ...), kind=kOutput, calls=%fused_computation.6.clone.1 | convolution fusion | flops 1218445312 | bytes 5643280 | tf_op jit(solution)/shard_map/while/body/eval_jaxpr/dot_general | solution.py:38
  190.7 0.0 copy-start.2
  190.7 8.4 %convolution_add_fusion.2 = f32[1024,1152]{1,0:T(8,128)} fusion(f32[1024,1152]{1,0:T(8,128)} %get-tuple-element.249, pred[]{:T(512)S(6)} %compare.3, bf16[4,512,1152]{2,1,0:T(8,128)(2,1)} %get-tuple-element.270, s32[]{:T(128)S(6)} %copy.17, f32[512,1024]{1,0:T(8,128)} %get-tuple-element.230, f32[]{:T(128)} %get-tuple-element.272, ...), kind=kOutput, calls=%fused_computation.2.clone.1 | convolution fusion | flops 1216086016 | bytes 12721157 | tf_op jit(solution)/shard_map/while/body/eval_jaxpr/dot_general | solution.py:47
  199.1 0.0 copy-done.2
  199.1 4.2 %fusion.31 = f32[4,512,1152]{2,1,0:T(8,128)} fusion(f32[4,512,1152]{2,1,0:T(8,128)} %get-tuple-element.253, s32[]{:T(128)S(6)} %copy.17, bf16[1024,1152]{1,0:T(8,128)(2,1)S(1)} %get-tuple-element.271, f32[512,1024]{1,0:T(8,128)S(1)} %copy-done.2, f32[]{:T(128)} %get-tuple-element.272, f32[]{:T(128)} %get-tuple-element.269, ...), kind=kOutput, calls=%fused_computation.4.clone.1 | convolution fusion | flops 1213726720 | bytes 6822916 | tf_op jit(solution)/shard_map/while/body/eval_jaxpr/dot_general | solution.py:46
  203.3 4.8 %broadcast_multiply_fusion.1 = f32[1024,1152]{1,0:T(8,128)} fusion(f32[1024,1152]{1,0:T(8,128)} %get-tuple-element.73, f32[]{:T(128)} %exp.10), kind=kLoop, calls=%fused_computation.29 | loop fusion | flops 1179648 | bytes 9437188 | tf_op jit(solution)/shard_map/mul | solution.py:67
  208.1 0.0 reduce-scatter.5.cloned.1.call-update
  208.2 0.2 reduce-scatter.3.cloned.1.call-start
  208.4 8.0 %broadcast_multiply_fusion = f32[4,512,1152]{2,1,0:T(8,128)} fusion(f32[4,512,1152]{2,1,0:T(8,128)} %get-tuple-element.72, f32[]{:T(128)} %exp.10), kind=kLoop, calls=%fused_computation.28 | loop fusion | flops 2359296 | bytes 18874372 | tf_op jit(solution)/shard_map/mul | solution.py:66
  216.4 0.0 reduce-scatter.3.cloned.1.call-update
  216.4 0.1 dynamic-slice.7
  216.5 74.4 %all-reduce = (f32[]{:T(128)}, f32[]{:T(128)}, f32[]{:T(128)}) all-reduce(f32[]{:T(128)} %get-tuple-element.71, f32[]{:T(128)} %get-tuple-element.74, f32[]{:T(128)} %get-tuple-element.75), channel_id=1, replica_groups=mesh['img'=8,'txt'=16] {'img','txt'}, use_global_device_ids=true, to_apply=%region_7.8 | all-reduce | flops 3 | bytes 24 | tf_op jit(solution)/shard_map/psum | solution.py:80
  290.9 0.1 dynamic-slice.6
  292.3 5.1 %reduce-scatter.5.cloned.1.call-done = f32[128,1152]{1,0:T(8,128)} async-done(((f32[1024,1152]{1,0:T(8,128)}), f32[128,1152]{1,0:T(8,128)}) %reduce-scatter.5.cloned.1.call-update) | async-done | bytes 589840 | tf_op jit(solution)/shard_map/reduce_scatter | solution.py:77
  297.4 1.4 multiply_reduce_fusion.1
  298.7 2.2 subtract_divide_fusion
  301.0 74.0 %reduce-scatter.3.cloned.1.call-done = f32[128,1152]{1,0:T(8,128)} async-done(((f32[2048,1152]{1,0:T(8,128)}), f32[128,1152]{1,0:T(8,128)}) %reduce-scatter.3.cloned.1.call-update) | async-done | bytes 589840 | tf_op jit(solution)/shard_map/reduce_scatter | solution.py:76
  375.0 1.4 multiply_reduce_fusion.2
  376.4 2.2 subtract_divide_fusion.1
  (12 shorter events, 0.1 us)
Async XLA Ops:
  7.2 62.0 %all-gather.5.cloned.1.call-start = ((), (), s32[]{:S(2)}) async-start(), calls=%async_computation.3 | async-start | bytes 2654208 | tf_op jit(solution)/shard_map/all_gather | solution.py:23
  7.9 99.2 %all-gather.3.cloned.1.call-start = ((), (), s32[]{:S(2)}) async-start(), calls=%async_computation.2 | async-start | bytes 5013504 | tf_op jit(solution)/shard_map/all_gather | solution.py:22
  8.6 288.7 %reduce-scatter.5.cloned.1.call-start = ((), (), s32[]{:S(2)}) async-start(), calls=%async_computation.5 | async-start | bytes 5308416 | tf_op jit(solution)/shard_map/reduce_scatter | solution.py:77
  69.2 2.4 copy-start.1
  107.1 3.8 copy-start
  126.8 7.0 %copy-start.2 = (f32[512,1024]{1,0:T(8,128)S(1)}, f32[512,1024]{1,0:T(8,128)}, u32[]{:S(2)}) copy-start(f32[512,1024]{1,0:T(8,128)} %get-tuple-element.230) | copy-start | bytes 6291460 | tf_op jit(solution)/shard_map/while
  147.1 8.4 %copy-start.2 = (f32[512,1024]{1,0:T(8,128)S(1)}, f32[512,1024]{1,0:T(8,128)}, u32[]{:S(2)}) copy-start(f32[512,1024]{1,0:T(8,128)} %get-tuple-element.230) | copy-start | bytes 6291460 | tf_op jit(solution)/shard_map/while
  169.0 8.4 %copy-start.2 = (f32[512,1024]{1,0:T(8,128)S(1)}, f32[512,1024]{1,0:T(8,128)}, u32[]{:S(2)}) copy-start(f32[512,1024]{1,0:T(8,128)} %get-tuple-element.230) | copy-start | bytes 6291460 | tf_op jit(solution)/shard_map/while
  190.7 8.4 %copy-start.2 = (f32[512,1024]{1,0:T(8,128)S(1)}, f32[512,1024]{1,0:T(8,128)}, u32[]{:S(2)}) copy-start(f32[512,1024]{1,0:T(8,128)} %get-tuple-element.230) | copy-start | bytes 6291460 | tf_op jit(solution)/shard_map/while
  208.2 166.8 %reduce-scatter.3.cloned.1.call-start = ((), (), s32[]{:S(2)}) async-start(), calls=%async_computation.4 | async-start | bytes 10027008 | tf_op jit(solution)/shard_map/reduce_scatter | solution.py:76
Sparse Core Ops, SparseCore 0:
  10.3 58.8 all-gather.4
  70.9 36.0 all-gather.2
  208.3 89.0 reduce-scatter.4
  299.6 75.2 reduce-scatter.2
where the time goes:
time: 388 us; the launch traced here: 387 us
  waiting for transfers between devices  172 us (44%)
  matrix products  77.8 us (20%)
  blocking collectives  74.4 us (19%)
  other arithmetic  35.5 us (9%)
  between operations  18.1 us (5%)
  loops' own time  7.85 us (2%)
    psum x1, blocking collectives, body(): lax.psum((loss_part, weight_part, cos_part), ('img', 'txt'))  74.4 us
    reduce_scatter x1, waiting for transfers between devices, body(): lax.psum_scatter(image_partial, 'txt', scatter_dimension=0, tiled=True)  74 us
    all_gather x1, waiting for transfers between devices, body(): text_full = lax.all_gather(text_emb, 'img', axis=0, tiled=True)  59.1 us
    all_gather x1, waiting for transfers between devices, body(): image_full = lax.all_gather(image_emb, 'txt', axis=0, tiled=True)  32.6 us
    dot_general x4, matrix products, step(): lax.dot_general(weight_low, rows_low, (((0,), (0,)), ((), ())), preferred...  32 us
    dot_general x4, matrix products, step(): lax.dot_general(rows_low, text_low, (((1,), (1,)), ((), ())), preferred_e...  28.9 us
    dot_general x4, matrix products, step(): jnp.dot(weight_low, text_low, preferred_element_type=jnp.float32)  16.9 us
    div x2, other arithmetic, unit_rows(): return (values / norm, norm)  9.66 us
  transfers between devices with their start and end apart: 4, of which 4 were waited for; matrix products, arithmetic and copies ran while one was open for 5% of the time, Pallas kernels for 0%

commit v1 on v0

v1 whole, which is shorter than its diff:
```python
import jax
import jax.numpy as jnp
from jax import lax
from jax.experimental import pallas as pl
from jax.experimental.pallas import tpu as pltpu
from jax.sharding import PartitionSpec as P

EPS = 1e-06
LOG2E = 1.4426950408889634
MESH = pl.DeviceIdType.MESH
OWN, PAIR = 0, 1
ROWS = 128
HALF = ROWS // 2
PLUS, MINUS = 0, 1

NAMES = []
for _kind in ("image", "text"):
    NAMES += [(_kind, "y", h) for h in (0, 1)]
    NAMES += [(_kind, step, way, h) for step in ("own", "pair") for way in (PLUS, MINUS) for h in (0, 1)]
    NAMES += [(_kind, step, way) for step in ("own2", "pair2") for way in (PLUS, MINUS)]
    NAMES += [(_kind, "far", way, t) for way in (PLUS, MINUS) for t in (OWN, PAIR)]
    NAMES += [(_kind, "near", way, t) for way in (PLUS, MINUS) for t in (OWN, PAIR)]
    NAMES += [(_kind, "home")]
NAMES += [("core", t, d) for t in (OWN, PAIR) for d in range(4)]
NAMES += [("coresum", t, d) for t in (OWN, PAIR) for d in range(4)]
NAMES += [("sum", stage) for stage in ("core", "y", "yy")]
NAMES += [("sum", axis, d) for axis in ("x", "z") for d in (1, 2, 3)]
IDS = {name: i for i, name in enumerate(NAMES)}


def unit_rows(emb):
    values = emb.astype(jnp.float32)
    norm = jnp.sqrt(jnp.sum(values * values, axis=1, keepdims=True) + EPS)
    return values / norm, norm


class Ring:
    def __init__(self, kind, rows, partner, plus, minus, slot):
        self.kind, self.rows, self.partner = kind, rows, partner
        self.to = {PLUS: plus, MINUS: minus}
        self.slot = slot

    def part(self, t, d, h):
        return self.rows.at[pl.ds(pl.multiple_of(self.slot(t, d) * ROWS + h * HALF, HALF), HALF)]


def kernel(
    image_emb, text_emb, positive, log_scale, bias,
    loss_ref, image_grad, text_grad, scale_grad, bias_grad,
    image_rows, text_rows, weight, weight_t, image_unit, text_unit, image_norm, text_norm,
    image_own, text_own, core_out, core_in,
    image_far_out, image_far_in, image_near_out, image_near_in, image_home_out, image_home_in,
    text_far_out, text_far_in, text_near_out, text_near_in, text_home_out, text_home_in,
    totals, sums, sums_in, ring_sums, send_sem, recv_sem,
):
    img, txt = lax.axis_index("img"), lax.axis_index("txt")
    z, yh = lax.div(img, 2), lax.rem(img, 2)
    yl, x, c = lax.div(txt, 8), lax.rem(lax.div(txt, 2), 4), lax.rem(txt, 2)

    def device(z=z, yh=yh, yl=yl, x=x, c=c):
        return (z * 2 + yh, yl * 8 + x * 2 + c)

    def step(i, d):
        return lax.rem(i + d, 4)

    sibling = device(c=1 - c)
    image_partner = device(yl=1 - yl)
    text_partner = device(yl=1 - yl, yh=1 - yh)
    x_at = {d: device(x=step(x, d)) for d in (1, 2, 3)}
    z_at = {d: device(z=step(z, d)) for d in (1, 2, 3)}

    barrier = pltpu.get_barrier_semaphore()
    partners = [sibling, image_partner, text_partner, *x_at.values(), *z_at.values()]
    for partner in partners:
        pl.semaphore_signal(barrier, inc=1, device_id=partner, device_id_type=MESH)

    def image_slot(t, d, core=c):
        return (yl + t * (1 - 2 * yl)) * 8 + step(x, d) * 2 + core

    def text_slot(t, d):
        return step(z, d) * 2 + (yh + t * (1 - 2 * yh))

    image = Ring("image", image_rows, image_partner, x_at[1], x_at[3], image_slot)
    text = Ring("text", text_rows, text_partner, z_at[1], z_at[3], text_slot)

    started = []

    def send(name, src, dst, to):
        i = IDS[name]
        copy = pltpu.make_async_remote_copy(
            src_ref=src, dst_ref=dst, send_sem=send_sem.at[i], recv_sem=recv_sem.at[i], device_id=to, device_id_type=MESH
        )
        copy.start()
        started.append(copy)

    def recv(name, dst):
        i = IDS[name]
        pltpu.make_async_remote_copy(
            src_ref=dst, dst_ref=dst, send_sem=send_sem.at[i], recv_sem=recv_sem.at[i], device_id=sibling, device_id_type=MESH
        ).wait_recv()

    def block(slot):
        return pl.ds(pl.multiple_of(slot * ROWS, ROWS), ROWS)

    def own_rows(emb, ring, unit_ref, norm_ref):
        unit, norm = unit_rows(emb[...])
        unit_ref[...] = unit
        norm_ref[...] = norm
        ring.rows[block(ring.slot(OWN, 0)), :] = unit.astype(jnp.bfloat16)

    own_rows(image_emb, image, image_unit, image_norm)
    own_rows(text_emb, text, text_unit, text_norm)
    pl.semaphore_wait(barrier, len(partners))

    def forward(ring, name, t, d, h, to):
        part = ring.part(t, d, h)
        send((ring.kind, *name), part, part, to)

    def arrived(ring, name, t, d, h):
        recv((ring.kind, *name), ring.part(t, d, h))

    def to_sibling(t, d):
        part = image_rows.at[block(image_slot(t, d))]
        send(("core", t, d), part, part, sibling)

    def from_sibling(t, d):
        recv(("core", t, d), image_rows.at[block(image_slot(t, d, 1 - c))])

    def gather_start(ring):
        for h in (0, 1):
            forward(ring, ("y", h), OWN, 0, h, ring.partner)
            forward(ring, ("own", PLUS, h), OWN, 0, h, ring.to[PLUS])
            forward(ring, ("own", MINUS, 1 - h), OWN, 0, 1 - h, ring.to[MINUS])

    def gather_first(ring):
        arrived(ring, ("own", PLUS, 0), OWN, 3, 0)
        forward(ring, ("own2", PLUS), OWN, 3, 0, ring.to[PLUS])
        arrived(ring, ("own", MINUS, 1), OWN, 1, 1)
        forward(ring, ("own2", MINUS), OWN, 1, 1, ring.to[MINUS])
        arrived(ring, ("y", 0), PAIR, 0, 0)
        for way in (PLUS, MINUS):
            forward(ring, ("pair", way, 0), PAIR, 0, 0, ring.to[way])

    def gather_second(ring):
        arrived(ring, ("y", 1), PAIR, 0, 1)
        for way in (PLUS, MINUS):
            forward(ring, ("pair", way, 1), PAIR, 0, 1, ring.to[way])
        arrived(ring, ("own", PLUS, 1), OWN, 3, 1)
        arrived(ring, ("own", MINUS, 0), OWN, 1, 0)

    def gather_third(ring):
        arrived(ring, ("pair", PLUS, 0), PAIR, 3, 0)
        forward(ring, ("pair2", PLUS), PAIR, 3, 0, ring.to[PLUS])
        arrived(ring, ("pair", MINUS, 1), PAIR, 1, 1)
        forward(ring, ("pair2", MINUS), PAIR, 1, 1, ring.to[MINUS])
        arrived(ring, ("pair", PLUS, 1), PAIR, 3, 1)
        arrived(ring, ("pair", MINUS, 0), PAIR, 1, 0)

    def gather_last(ring):
        arrived(ring, ("own2", PLUS), OWN, 2, 0)
        arrived(ring, ("own2", MINUS), OWN, 2, 1)
        arrived(ring, ("pair2", PLUS), PAIR, 2, 0)
        arrived(ring, ("pair2", MINUS), PAIR, 2, 1)

    scale = jnp.exp(jnp.full((1, 128), log_scale[0], jnp.float32))
    scale2 = jnp.concatenate([scale * LOG2E] * 2, axis=1)
    bias2 = jnp.full((1, 256), bias[0] * LOG2E, jnp.float32)
    totals[...] = jnp.zeros_like(totals)

    def fold(values):
        return values[:, :128] + values[:, 128:]

    def tile(dz, t, dx):
        zt = step(z, dz)
        start = pl.multiple_of(zt * 256, 256)
        columns = pl.multiple_of(image_slot(t, dx, 0) * ROWS, 256)
        cosine = lax.dot_general(
            text_rows[pl.ds(start, 256), :], image_rows[pl.ds(columns, 256), :],
            (((1,), (1,)), ((), ())), preferred_element_type=jnp.float32,
        )
        wanted = positive[:, pl.ds(columns, 256)]
        add = [jnp.zeros((8, 256), jnp.float32) for _ in range(4)]
        for q in (0, 1):
            lo = yl + (q - yh) * (q - yh) * (1 - 2 * yl)
            first = ((lo * 8 + x * 2 + c) * 8 + zt * 2 + q) * ROWS
            for part in (0, 1):
                rows = slice(q * ROWS + part * HALF, q * ROWS + (part + 1) * HALF)
                cos = cosine[rows]
                row = lax.broadcasted_iota(jnp.int32, (HALF, 256), 0)
                hot = (row == wanted - (first + part * HALF)).astype(jnp.float32)
                e = jnp.exp2(cos * scale2 + bias2)
                u = 1.0 + e
                w = e / u - hot
                weight_t[pl.ds(pl.multiple_of(start + rows.start, HALF), HALF), pl.ds(columns, 256)] = w.astype(jnp.bfloat16)
                e8, u8 = e.reshape(8, 8, 256), u.reshape(8, 8, 256)
                product = e8[0]
                for k in range(1, 8):
                    product = product * u8[k] + e8[k]
                add[0] += jnp.log1p(product)
                add[1] += jnp.sum(w.reshape(8, 8, 256), axis=0)
                add[2] += jnp.sum((w * cos).reshape(8, 8, 256), axis=0)
                add[3] += jnp.sum((hot * cos).reshape(8, 8, 256), axis=0)
            at = pl.multiple_of(start + q * ROWS, ROWS)
            weight[pl.ds(columns, 256), pl.ds(at, ROWS)] = weight_t[pl.ds(at, ROWS), pl.ds(columns, 256)].T
        for i in range(4):
            totals[i] += fold(add[i])

    def tiles(count, place):
        def body(i, carry):
            tile(*place(i))
            return carry

        lax.fori_loop(0, count, body, 0)

    def three(i):
        return lax.div(i * (i + 1), 2)

    gather_start(image)
    gather_start(text)
    to_sibling(OWN, 0)
    gather_first(image)
    gather_first(text)
    gather_second(image)
    gather_second(text)
    to_sibling(OWN, 3)
    to_sibling(OWN, 1)
    to_sibling(PAIR, 0)
    for t, d in ((OWN, 0), (OWN, 3), (OWN, 1), (PAIR, 0)):
        from_sibling(t, d)
    tiles(2, lambda i: (0, i, 0))
    tiles(2, lambda i: (0, OWN, 1 + 2 * i))
    gather_third(image)
    gather_third(text)
    to_sibling(PAIR, 3)
    to_sibling(PAIR, 1)
    for d in (3, 1):
        from_sibling(PAIR, d)
    tiles(2, lambda i: (0, PAIR, 1 + 2 * i))
    tiles(12, lambda i: (1 + 2 * lax.div(i, 6), lax.rem(i, 2), three(lax.rem(lax.div(i, 2), 3))))
    gather_last(image)
    to_sibling(OWN, 2)
    to_sibling(PAIR, 2)
    gather_last(text)
    from_sibling(OWN, 2)
    from_sibling(PAIR, 2)
    tiles(8, lambda i: (lax.rem(i, 4), lax.div(i, 4), 2))

    def place(t, d):
        return t * 4 + d

    def image_parts(blocks):
        lhs = []
        for t, d in blocks:
            lhs += [weight[block(image_slot(t, d)), :], weight[block(image_slot(t, d, 1 - c)), :]]
        out = jnp.dot(jnp.concatenate(lhs, axis=0), text_rows[...], preferred_element_type=jnp.float32)
        for n, (t, d) in enumerate(blocks):
            image_own[place(t, d)] = out[n * 256 : n * 256 + ROWS]
            core_out[place(t, d)] = out[n * 256 + ROWS : (n + 1) * 256].astype(jnp.bfloat16)
            send(("coresum", t, d), core_out.at[place(t, d)], core_in.at[place(t, d)], sibling)

    def text_parts(steps):
        blocks = [(t, d) for d in steps for t in (PAIR, OWN)]
        lhs = [weight_t[block(text_slot(t, d)), :] for t, d in blocks]
        out = jnp.dot(jnp.concatenate(lhs, axis=0), image_rows[...], preferred_element_type=jnp.float32)
        for n, (t, d) in enumerate(blocks):
            text_own[place(t, d)] = out[n * ROWS : (n + 1) * ROWS]

    def image_part(t, d):
        recv(("coresum", t, d), core_in.at[place(t, d)])
        return image_own[place(t, d)] + core_in[place(t, d)].astype(jnp.float32)

    def text_part(t, d):
        return text_own[place(t, d)]

    def send_far(ring, part, out, into, t):
        value = part(t, 2).astype(jnp.bfloat16)
        for way in (PLUS, MINUS):
            out[t, way] = value[way * HALF : (way + 1) * HALF]
            send((ring.kind, "far", way, t), out.at[t, way], into.at[t, way], ring.to[way])

    def send_near(ring, part, far_in, out, into, t):
        for way in (PLUS, MINUS):
            value = part(t, 1 if way == PLUS else 3)
            recv((ring.kind, "far", way, t), far_in.at[t, way])
            mine = slice(way * HALF, (way + 1) * HALF)
            other = slice((1 - way) * HALF, (2 - way) * HALF)
            out[t, way, mine] = (value[mine] + far_in[t, way].astype(jnp.float32)).astype(jnp.bfloat16)
            out[t, way, other] = value[other].astype(jnp.bfloat16)
            send((ring.kind, "near", way, t), out.at[t, way], into.at[t, way], ring.to[way])

    def ring_sum(ring, part, near_in, t):
        value = part(t, 0)
        for way in (PLUS, MINUS):
            recv((ring.kind, "near", way, t), near_in.at[t, way])
            value = value + near_in[t, way].astype(jnp.float32)
        return value

    def send_home(ring, part, near_in, out, into):
        out[...] = ring_sum(ring, part, near_in, PAIR).astype(jnp.bfloat16)
        send((ring.kind, "home"), out, into, ring.partner)

    def finish(ring, part, near_in, home_in, unit_ref, norm_ref, grad):
        value = ring_sum(ring, part, near_in, OWN)
        recv((ring.kind, "home"), home_in)
        value = (value + home_in[...].astype(jnp.float32)) * scale[:, :1]
        unit = unit_ref[...]
        grad[...] = (value - unit * jnp.sum(unit * value, axis=1, keepdims=True)) / norm_ref[...]

    image_parts([(PAIR, 2), (OWN, 2)])
    tiles(6, lambda i: (2, lax.rem(i, 2), three(lax.div(i, 2))))
    for t in (PAIR, OWN):
        send_far(image, image_part, image_far_out, image_far_in, t)

    for i in range(4):
        sums[0, i : i + 1] = jnp.sum(totals[i], axis=0, keepdims=True)
    sums[0, 4:] = jnp.zeros((4, 128), jnp.float32)
    send(("sum", "core"), sums.at[0], sums_in.at[0], sibling)

    text_parts([2])
    for t in (PAIR, OWN):
        send_far(text, text_part, text_far_out, text_far_in, t)

    def next_sum(i, name):
        recv(("sum", name), sums_in.at[i])
        sums[i + 1] = sums[i] + sums_in[i]

    next_sum(0, "core")
    send(("sum", "y"), sums.at[1], sums_in.at[1], image_partner)

    image_parts([(PAIR, 1), (PAIR, 3)])
    text_parts([1, 3])
    send_near(image, image_part, image_far_in, image_near_out, image_near_in, PAIR)
    send_near(text, text_part, text_far_in, text_near_out, text_near_in, PAIR)
    next_sum(1, "y")
    send(("sum", "yy"), sums.at[2], sums_in.at[2], text_partner)

    image_parts([(OWN, 1), (OWN, 3)])
    send_near(text, text_part, text_far_in, text_near_out, text_near_in, OWN)
    send_near(image, image_part, image_far_in, image_near_out, image_near_in, OWN)
    next_sum(2, "yy")

    def share(i, axis, me, at, source):
        ring_sums[i, me] = sums[source]
        for d in (1, 2, 3):
            send(("sum", axis, d), sums.at[source], ring_sums.at[i, me], at[d])

    def shared(i, axis, me, into):
        for d in (1, 2, 3):
            recv(("sum", axis, d), ring_sums.at[i, step(me, 4 - d)])
        sums[into] = (ring_sums[i, 0] + ring_sums[i, 1]) + (ring_sums[i, 2] + ring_sums[i, 3])

    share(0, "x", x, x_at, 3)
    image_parts([(PAIR, 0), (OWN, 0)])
    text_parts([0])
    shared(0, "x", x, 4)
    share(1, "z", z, z_at, 4)

    send_home(image, image_part, image_near_in, image_home_out, image_home_in)
    send_home(text, text_part, text_near_in, text_home_out, text_home_in)
    shared(1, "z", z, 5)
    finish(image, image_part, image_near_in, image_home_in, image_unit, image_norm, image_grad)
    finish(text, text_part, text_near_in, text_home_in, text_unit, text_norm, text_grad)

    total = jnp.sum(sums[5], axis=1, keepdims=True)
    pairs = positive.shape[1] * 8
    factor = scale[:, :1]
    loss_ref[...] = (total[0:1] - factor * total[3:4]) / pairs - bias[0]
    scale_grad[...] = factor * total[2:3]
    bias_grad[...] = total[1:2]
    for copy in started:
        copy.wait_send()


def body(image_emb, text_emb, positive, log_scale, bias):
    rows, width = image_emb.shape
    images, texts = 16 * rows, 8 * rows
    low, full = jnp.bfloat16, jnp.float32
    vmem = pl.BlockSpec(memory_space=pltpu.VMEM)
    smem = pl.BlockSpec(memory_space=pltpu.SMEM)
    scalar = jax.ShapeDtypeStruct((1, 1), full)
    grad = jax.ShapeDtypeStruct((rows, width), full)
    sums_home = [
        pltpu.VMEM((2, 2, HALF, width), low), pltpu.VMEM((2, 2, HALF, width), low),
        pltpu.VMEM((2, 2, rows, width), low), pltpu.VMEM((2, 2, rows, width), low),
        pltpu.VMEM((rows, width), low), pltpu.VMEM((rows, width), low),
    ]
    loss, image_grad, text_grad, scale_grad, bias_grad = pl.pallas_call(
        kernel,
        out_shape=(scalar, grad, grad, scalar, scalar),
        in_specs=[vmem, vmem, vmem, smem, smem],
        out_specs=(vmem,) * 5,
        scratch_shapes=[
            pltpu.VMEM((images, width), low),
            pltpu.VMEM((texts, width), low),
            pltpu.VMEM((images, texts), low),
            pltpu.VMEM((texts, images), low),
            pltpu.VMEM((rows, width), full),
            pltpu.VMEM((rows, width), full),
            pltpu.VMEM((rows, 1), full),
            pltpu.VMEM((rows, 1), full),
            pltpu.VMEM((8, rows, width), full),
            pltpu.VMEM((8, rows, width), full),
            pltpu.VMEM((8, rows, width), low),
            pltpu.VMEM((8, rows, width), low),
            *sums_home,
            *sums_home,
            pltpu.VMEM((4, 8, 128), full),
            pltpu.VMEM((6, 8, 128), full),
            pltpu.VMEM((3, 8, 128), full),
            pltpu.VMEM((2, 4, 8, 128), full),
            pltpu.SemaphoreType.DMA((len(NAMES),)),
            pltpu.SemaphoreType.DMA((len(NAMES),)),
        ],
        compiler_params=pltpu.CompilerParams(collective_id=0, has_side_effects=True, vmem_limit_bytes=56 * 2**20),
    )(image_emb, text_emb, positive.reshape(1, images), log_scale.reshape(1), bias.reshape(1))
    return loss.reshape(()), image_grad, text_grad, scale_grad.reshape(()), bias_grad.reshape(())


def solution(mesh):
    placed = (P(("img", "txt"), None), P(("txt", "img"), None), P("img"), P(), P())
    return jax.shard_map(
        body,
        mesh=mesh,
        in_specs=placed,
        out_specs=(P(), P(("img", "txt"), None), P(("txt", "img"), None), P(), P()),
        check_vma=False,
    )
```

time: 388 us -> 89.7 us (0.23)
  waiting for transfers between devices: 172 us -> 0 us
  Pallas kernels: 0 us -> 79.6 us
  matrix products: 77.8 us -> 0 us
  blocking collectives: 74.4 us -> 0 us
  other arithmetic: 35.5 us -> 0 us
  between operations: 18.1 us -> 7.13 us
  loops' own time: 7.85 us -> 0 us
    all_gather x2 -> x0, waiting for transfers between devices: 91.7 us -> none  [the longest x1 59.1 us: body(): text_full = lax.all_gather(text_emb, 'img', axis=0, tiled=True)]
    pallas_call x0 -> x1, Pallas kernels: none -> 79.6 us  [body(): pl.pallas_call(kernel, out_shape=(scalar, grad, grad, scalar, scalar), in...]
    reduce_scatter x2 -> x0, waiting for transfers between devices: 79.1 us -> none  [the longest x1 74 us: body(): lax.psum_scatter(image_partial, 'txt', scatter_dimension=0, tiled=True)]
    dot_general x12 -> x0, matrix products: 77.8 us -> none  [the longest x4 32 us: step(): lax.dot_general(weight_low, rows_low, (((0,), (0,)), ((), ())), preferred...]
    psum x1 -> x0, blocking collectives: 74.4 us -> none  [body(): lax.psum((loss_part, weight_part, cos_part), ('img', 'txt'))]
    div x4 -> x0, other arithmetic: 14.1 us -> none  [the longest x2 9.66 us: unit_rows(): return (values / norm, norm)]
    mul x2 -> x0, other arithmetic: 12.9 us -> none  [the longest x1 8.02 us: body(): image_partial = scale * image_parts.reshape(image_rows, width)]
    reduce_sum x4 -> x0, other arithmetic: 8.57 us -> none  [the longest x2 5.82 us: unit_rows(): norm = jnp.sqrt(jnp.sum(values * values, axis=1, keepdims=True) + EPS)]
  transfers between devices with their start and end apart: 4 -> 0, of which waited for: 4 -> 0; matrix products, arithmetic and copies ran while one was open for 5% -> 0% of each run, Pallas kernels for 0% -> 0%
where the time goes in v1:
time: 89.7 us; the launch traced here: 89.5 us
  Pallas kernels  79.6 us (89%)
  between operations  7.13 us (8%)
  local copies, waits for them, and re-layouts  2.8 us (3%)
    pallas_call x1, Pallas kernels, body(): pl.pallas_call(kernel, out_shape=(scalar, grad, grad, scalar, scalar), in...  79.6 us
    unnamed x4, local copies, waits for them, and re-layouts  2.8 us

profile of v1, /device:TPU:0, one launch (start us, length us, event | category | flops | bytes accessed | tf_op | source)
XLA Modules:
  0.0 89.5 jit_solution(6439641768393428704)
XLA Ops:
  1.9 79.6 %shard_map.92 = (f32[1,1]{1,0:T(1,128)}, f32[128,1152]{1,0:T(8,128)}, f32[128,1152]{1,0:T(8,128)}, f32[1,1]{1,0:T(1,128)}, f32[1,1]{1,0:T(1,128)}) custom-call(bf16[128,1152]{1,0:T(8,128)(2,1)} %image_emb.1, bf16[128,1152]{1,0:T(8,128)(2,1)} %text_emb.1, s32[1,2048]{1,0:T(1,128)} %bitcast.8, f32[1]{0:T(128)} %bitcast.6.log_scale, f32[1]{0:T(128)} %bitcast.7.bias), custom_call_target="tpu_custom_call" | custom-call | tf_op jit(solution)/shard_map/pallas_call | solution.py:387
  82.1 0.0 copy-start
  82.1 2.0 %copy.18 = f32[128,1152]{1,0:T(8,128)} copy(f32[128,1152]{1,0:T(8,128)} %get-tuple-element.21) | data formatting | bytes 1179648
  84.1 0.0 copy-done
  84.1 0.8 copy.19
Async XLA Ops:
  82.1 2.0 %copy-start = (f32[128,1152]{1,0:T(8,128)S(1)}, f32[128,1152]{1,0:T(8,128)}, u32[]{:S(2)}) copy-start(f32[128,1152]{1,0:T(8,128)} %get-tuple-element.22) | copy-start | bytes 1769476

commit v2 on v0

v2 whole, which is shorter than its diff:
```python
import jax
import jax.numpy as jnp
from jax import lax
from jax.experimental import pallas as pl
from jax.experimental.pallas import tpu as pltpu
from jax.sharding import PartitionSpec as P

EPS = 1e-06
LOG2E = 1.4426950408889634
MESH = pl.DeviceIdType.MESH
OWN, PAIR = 0, 1
ROWS = 128
HALF = ROWS // 2
QUARTER = ROWS // 4
PLUS, MINUS = 0, 1
OWN_A, OWN_B, PAIR_A = 0, 1, 2
FIRST = [(OWN, 0), (PAIR, 0), (OWN, 1), (OWN, 3)]
SECOND = [(PAIR, 1), (PAIR, 3), (OWN, 2)]
LAST = [(PAIR, 2)]

NAMES = []
for _kind in ("image", "text"):
    NAMES += [(_kind, "y", h) for h in (0, 1)]
    NAMES += [(_kind, "y_ring", d) for d in (1, 2, 3)]
    NAMES += [(_kind, "own", way, h) for way in (PLUS, MINUS) for h in (0, 1)]
    NAMES += [(_kind, "own2", way, h) for way in (PLUS, MINUS) for h in (0, 1)]
    NAMES += [(_kind, step, way) for step in ("pair", "pair2") for way in (PLUS, MINUS)]
    NAMES += [(_kind, "y_sum", d) for d in range(4)]
    NAMES += [(_kind, step, way, part) for step in ("far", "near") for way in (PLUS, MINUS) for part in range(3)]
    NAMES += [(_kind, "home")]
NAMES += [("core", t, d) for t in (OWN, PAIR) for d in range(4)]
NAMES += [("coresum", t, d) for t in (OWN, PAIR) for d in range(4)]
NAMES += [("sum", stage) for stage in ("core", "y", "yy")]
NAMES += [("sum", axis, d) for axis in ("x", "z") for d in (1, 2, 3)]
IDS = {name: i for i, name in enumerate(NAMES)}


def unit_rows(emb):
    values = emb.astype(jnp.float32)
    norm = jnp.sqrt(jnp.sum(values * values, axis=1, keepdims=True) + EPS)
    return values / norm, norm


class Ring:
    def __init__(self, kind, rows, partner, plus, minus, slot):
        self.kind, self.rows, self.partner = kind, rows, partner
        self.to = {PLUS: plus, MINUS: minus}
        self.slot = slot

    def part(self, t, d, first, count):
        return self.rows.at[pl.ds(pl.multiple_of(self.slot(t, d) * ROWS + first, QUARTER), count)]


class Home:
    def __init__(self, own, far_out, far_in, near_out, near_in, y_out, y_in, home_out, home_in):
        self.own, self.far_out, self.far_in, self.near_out, self.near_in = own, far_out, far_in, near_out, near_in
        self.y_out, self.y_in, self.home_out, self.home_in = y_out, y_in, home_out, home_in


def kernel(
    image_emb, text_emb, positive_in, log_scale, bias,
    image_sum, text_sum, scalar_sums,
    image_in, text_in, positive, image_rows, text_rows, weight_t, core_out, core_in, *rest,
):
    image_home, text_home = Home(*rest[:9]), Home(*rest[9:18])
    totals, sums, sums_in, ring_sums, send_sem, recv_sem, load_sem = rest[18:]
    img, txt = lax.axis_index("img"), lax.axis_index("txt")
    z, yh = lax.div(img, 2), lax.rem(img, 2)
    yl, x, c = lax.div(txt, 8), lax.rem(lax.div(txt, 2), 4), lax.rem(txt, 2)

    loads = [
        pltpu.make_async_copy(src, dst, load_sem.at[i])
        for i, (src, dst) in enumerate(((image_emb, image_in), (text_emb, text_in), (positive_in, positive)))
    ]
    for load in loads:
        load.start()

    def device(z=z, yh=yh, yl=yl, x=x, c=c):
        return (z * 2 + yh, yl * 8 + x * 2 + c)

    def step(i, d):
        return lax.rem(i + d, 4)

    def other(bit, t):
        return bit + t * (1 - 2 * bit)

    sibling = device(c=1 - c)
    image_partner = device(yl=1 - yl)
    text_partner = device(yl=1 - yl, yh=1 - yh)
    x_at = {d: device(x=step(x, d)) for d in (1, 2, 3)}
    z_at = {d: device(z=step(z, d)) for d in (1, 2, 3)}

    barrier = pltpu.get_barrier_semaphore()
    partners = [sibling, image_partner, text_partner, *x_at.values(), *z_at.values()]
    for partner in partners:
        pl.semaphore_signal(barrier, inc=1, device_id=partner, device_id_type=MESH)

    def image_slot(t, d, core=c):
        return other(yl, t) * 8 + step(x, d) * 2 + core

    def text_slot(t, d):
        return step(z, d) * 2 + other(yh, t)

    image = Ring("image", image_rows, image_partner, x_at[1], x_at[3], image_slot)
    text = Ring("text", text_rows, text_partner, z_at[1], z_at[3], text_slot)

    started = []

    def send(name, src, dst, to):
        i = IDS[name]
        copy = pltpu.make_async_remote_copy(
            src_ref=src, dst_ref=dst, send_sem=send_sem.at[i], recv_sem=recv_sem.at[i], device_id=to, device_id_type=MESH
        )
        copy.start()
        started.append(copy)

    def recv(name, dst):
        i = IDS[name]
        pltpu.make_async_remote_copy(
            src_ref=dst, dst_ref=dst, send_sem=send_sem.at[i], recv_sem=recv_sem.at[i], device_id=sibling, device_id_type=MESH
        ).wait_recv()

    def block(slot):
        return pl.ds(pl.multiple_of(slot * ROWS, ROWS), ROWS)

    def own_rows(load, emb, ring):
        load.wait()
        unit, _ = unit_rows(emb[...])
        ring.rows[block(ring.slot(OWN, 0)), :] = unit.astype(jnp.bfloat16)

    own_rows(loads[0], image_in, image)
    own_rows(loads[1], text_in, text)
    pl.semaphore_wait(barrier, len(partners))

    def forward(ring, name, t, d, first, count, to):
        part = ring.part(t, d, first, count)
        send((ring.kind, *name), part, part, to)

    def arrived(ring, name, t, d, first, count):
        recv((ring.kind, *name), ring.part(t, d, first, count))

    def to_sibling(blocks):
        for t, d in blocks:
            part = image_rows.at[block(image_slot(t, d))]
            send(("core", t, d), part, part, sibling)

    def from_sibling(blocks):
        for t, d in blocks:
            recv(("core", t, d), image_rows.at[block(image_slot(t, d, 1 - c))])

    def quarter(way, h):
        return h * HALF + way * QUARTER, QUARTER

    def near(way):
        return 3 if way == PLUS else 1

    def gather_start(ring):
        forward(ring, ("y", 0), OWN, 0, 0, HALF, ring.partner)
        for h in (1, 0):
            for way in (PLUS, MINUS):
                forward(ring, ("own", way, h), OWN, 0, h * HALF, HALF, ring.to[way])
        forward(ring, ("y", 1), OWN, 0, HALF, HALF, ring.partner)

    def gather_ring(ring, h):
        for way in (PLUS, MINUS):
            d = near(way)
            arrived(ring, ("own", way, h), OWN, d, h * HALF, HALF)
            forward(ring, ("own2", way, h), OWN, d, *quarter(way, h), ring.to[way])
            if h == 1:
                forward(ring, ("y_ring", d), OWN, d, HALF, HALF, ring.partner)

    def gather_pair(ring):
        arrived(ring, ("y", 0), PAIR, 0, 0, HALF)
        for way in (PLUS, MINUS):
            forward(ring, ("pair", way), PAIR, 0, 0, HALF, ring.to[way])

    def gather_far(ring):
        for way in (PLUS, MINUS):
            arrived(ring, ("own2", way, 1), OWN, 2, *quarter(way, 1))
        forward(ring, ("y_ring", 2), OWN, 2, HALF, HALF, ring.partner)

    def gather_pair_ring(ring):
        for way in (PLUS, MINUS):
            d = near(way)
            arrived(ring, ("pair", way), PAIR, d, 0, HALF)
            forward(ring, ("pair2", way), PAIR, d, *quarter(way, 0), ring.to[way])

    def gather_second(ring):
        for d in (1, 3):
            arrived(ring, ("y_ring", d), PAIR, d, HALF, HALF)
        for way in (PLUS, MINUS):
            arrived(ring, ("own2", way, 0), OWN, 2, *quarter(way, 0))

    def gather_last(ring):
        arrived(ring, ("y_ring", 2), PAIR, 2, HALF, HALF)
        for way in (PLUS, MINUS):
            arrived(ring, ("pair2", way), PAIR, 2, *quarter(way, 0))

    scale = jnp.exp(jnp.full((1, 256), log_scale[0], jnp.float32))
    scale2 = scale * LOG2E
    bias2 = jnp.full((1, 256), bias[0] * LOG2E, jnp.float32)
    totals[...] = jnp.zeros_like(totals)

    def tile(blocks, t, dx):
        columns = pl.multiple_of(image_slot(t, dx, 0) * ROWS, 256)
        cosine = lax.dot_general(
            jnp.concatenate([text_rows[block(text_slot(*b)), :] for b in blocks], axis=0),
            image_rows[pl.ds(columns, 256), :], (((1,), (1,)), ((), ())), preferred_element_type=jnp.float32,
        )
        wanted = positive[:, pl.ds(columns, 256)]
        add = [jnp.zeros((8, 256), jnp.float32) for _ in range(3)]
        for n, (tt, dz) in enumerate(blocks):
            at = text_slot(tt, dz) * ROWS
            first = ((other(yl, tt) * 8 + x * 2 + c) * 8 + text_slot(tt, dz)) * ROWS
            for part in (0, HALF):
                cos = cosine[n * ROWS + part : n * ROWS + part + HALF]
                row = lax.broadcasted_iota(jnp.int32, (HALF, 256), 0)
                flip = jnp.where(row == wanted - (first + part), -1.0, 1.0)
                e = jnp.exp2((cos * scale2 + bias2) * flip)
                u = 1.0 + e
                w = (e / u) * flip
                weight_t[pl.ds(pl.multiple_of(at + part, HALF), HALF), pl.ds(columns, 256)] = w.astype(jnp.bfloat16)
                e8, u8 = e.reshape(8, 8, 256), u.reshape(8, 8, 256)
                product = e8[0]
                for k in range(1, 8):
                    product = product * u8[k] + e8[k]
                add[0] += jnp.log1p(product)
                add[1] += jnp.sum(w.reshape(8, 8, 256), axis=0)
                add[2] += jnp.sum((w * cos).reshape(8, 8, 256), axis=0)
        for i in range(3):
            totals[i] += add[i][:, :128] + add[i][:, 128:]

    def tiles(blocks, count, place):
        def body(i, carry):
            tile(blocks, *place(i))
            return carry

        lax.fori_loop(0, count, body, 0)

    def first_place(i):
        return lax.rem(i, 2) * (1 - lax.div(i, 2)), lax.div(i * (i - 1), 2)

    def place(t, d):
        return t * 4 + d

    def image_parts(blocks):
        slots = [image_slot(t, d, core) for t, d in blocks for core in (c, 1 - c)]
        lhs = jnp.concatenate([weight_t[:, block(slot)] for slot in slots], axis=1)
        out = lax.dot_general(lhs, text_rows[...], (((0,), (0,)), ((), ())), preferred_element_type=jnp.float32)
        for n, (t, d) in enumerate(blocks):
            core_out[place(t, d)] = out[n * 256 + ROWS : (n + 1) * 256].astype(jnp.bfloat16)
            send(("coresum", t, d), core_out.at[place(t, d)], core_in.at[place(t, d)], sibling)
            image_home.own[place(t, d)] = out[n * 256 : n * 256 + ROWS]

    def text_parts(blocks):
        lhs = jnp.concatenate([weight_t[block(text_slot(t, d)), :] for t, d in blocks], axis=0)
        out = jnp.dot(lhs, image_rows[...], preferred_element_type=jnp.float32)
        for n, (t, d) in enumerate(blocks):
            text_home.own[place(t, d)] = out[n * ROWS : (n + 1) * ROWS]

    def image_ready(blocks):
        for t, d in blocks:
            recv(("coresum", t, d), core_in.at[place(t, d)])

    def image_part(t, d, half):
        rows = slice(half * HALF, (half + 1) * HALF)
        return image_home.own[place(t, d), rows] + core_in[place(t, d), rows].astype(jnp.float32)

    def text_part(t, d, half):
        return text_home.own[place(t, d), half * HALF : (half + 1) * HALF]

    class Sums:
        def __init__(self, ring, home, part):
            self.ring, self.home, self.part = ring, home, part

        def send(self, name, src, dst, to):
            send((self.ring.kind, *name), src, dst, to)

        def recv(self, name, dst):
            recv((self.ring.kind, *name), dst)

        def value(self, part, d):
            if part == OWN_B:
                self.recv(("y_sum", d), self.home.y_in.at[d])
                return self.part(OWN, d, 1) + self.home.y_in[d].astype(jnp.float32)
            return self.part(OWN if part == OWN_A else PAIR, d, 0)

        def send_y(self, d):
            self.home.y_out[d] = self.part(PAIR, d, 1).astype(jnp.bfloat16)
            self.send(("y_sum", d), self.home.y_out.at[d], self.home.y_in.at[d], self.ring.partner)

        def send_far(self, part):
            value = self.value(part, 2).astype(jnp.bfloat16)
            for way in (PLUS, MINUS):
                self.home.far_out[part, way] = value[way * QUARTER : (way + 1) * QUARTER]
                out, into = self.home.far_out.at[part, way], self.home.far_in.at[part, way]
                self.send(("far", way, part), out, into, self.ring.to[way])

        def send_near(self, part):
            for way in (PLUS, MINUS):
                value = self.value(part, 1 if way == PLUS else 3)
                self.recv(("far", way, part), self.home.far_in.at[part, way])
                mine = slice(way * QUARTER, (way + 1) * QUARTER)
                rest = slice((1 - way) * QUARTER, (2 - way) * QUARTER)
                more = self.home.far_in[part, way].astype(jnp.float32)
                self.home.near_out[part, way, mine] = (value[mine] + more).astype(jnp.bfloat16)
                self.home.near_out[part, way, rest] = value[rest].astype(jnp.bfloat16)
                out, into = self.home.near_out.at[part, way], self.home.near_in.at[part, way]
                self.send(("near", way, part), out, into, self.ring.to[way])

        def ring_sum(self, part):
            value = self.value(part, 0)
            for way in (PLUS, MINUS):
                self.recv(("near", way, part), self.home.near_in.at[part, way])
                value = value + self.home.near_in[part, way].astype(jnp.float32)
            return value

        def send_home(self):
            self.home.home_out[...] = self.ring_sum(PAIR_A).astype(jnp.bfloat16)
            self.send(("home",), self.home.home_out, self.home.home_in, self.ring.partner)

        def finish(self, out):
            out[HALF:] = self.ring_sum(OWN_B)
            value = self.ring_sum(OWN_A)
            self.recv(("home",), self.home.home_in)
            out[:HALF] = value + self.home.home_in[...].astype(jnp.float32)

    images, texts = Sums(image, image_home, image_part), Sums(text, text_home, text_part)

    def next_sum(i, name):
        recv(("sum", name), sums_in.at[i])
        sums[i + 1] = sums[i] + sums_in[i]

    def share(i, axis, me, at, source):
        ring_sums[i, me] = sums[source]
        for d in (1, 2, 3):
            send(("sum", axis, d), sums.at[source], ring_sums.at[i, me], at[d])

    def shared(i, axis, me, into):
        for d in (1, 2, 3):
            recv(("sum", axis, d), ring_sums.at[i, step(me, 4 - d)])
        sums[into] = (ring_sums[i, 0] + ring_sums[i, 1]) + (ring_sums[i, 2] + ring_sums[i, 3])

    gather_start(image)
    gather_start(text)
    to_sibling([(OWN, 0)])
    loads[2].wait()
    for ring in (image, text):
        gather_ring(ring, 1)
        gather_pair(ring)
    for ring in (image, text):
        gather_ring(ring, 0)
    for ring in (image, text):
        arrived(ring, ("y", 1), PAIR, 0, HALF, HALF)
    to_sibling(FIRST[1:])
    gather_far(image)
    gather_far(text)
    from_sibling(FIRST)
    tiles(FIRST, 4, first_place)
    gather_pair_ring(image)
    gather_pair_ring(text)
    gather_second(image)
    to_sibling(SECOND)
    gather_second(text)
    tiles(SECOND, 4, first_place)
    gather_last(image)
    to_sibling(LAST)
    gather_last(text)
    every = FIRST + SECOND + LAST
    from_sibling(SECOND)
    tile(every, OWN, 2)
    image_parts([(OWN, 2)])
    tiles(LAST, 2, lambda i: (i, 0))
    tiles(LAST, 2, lambda i: (OWN, 1 + 2 * i))
    from_sibling(LAST)
    tile(every, PAIR, 2)
    image_parts([(PAIR, 2)])
    image_ready([(OWN, 2)])
    images.send_far(OWN_A)
    tiles(every, 2, lambda i: (PAIR, 1 + 2 * i))
    image_ready([(PAIR, 2)])
    images.send_y(2)
    images.send_far(PAIR_A)

    for i in range(3):
        sums[0, i : i + 1] = jnp.sum(totals[i], axis=0, keepdims=True)
    sums[0, 3:] = jnp.zeros((5, 128), jnp.float32)
    send(("sum", "core"), sums.at[0], sums_in.at[0], sibling)

    text_parts([(PAIR, 2), (OWN, 2)])
    texts.send_y(2)
    texts.send_far(PAIR_A)
    texts.send_far(OWN_A)
    image_parts([(PAIR, 1), (PAIR, 3)])
    next_sum(0, "core")
    send(("sum", "y"), sums.at[1], sums_in.at[1], image_partner)
    text_parts([(PAIR, 1), (PAIR, 3)])
    texts.send_y(1)
    texts.send_y(3)
    image_ready([(PAIR, 1), (PAIR, 3)])
    images.send_y(1)
    images.send_y(3)
    images.send_near(PAIR_A)
    texts.send_near(PAIR_A)
    images.send_far(OWN_B)
    texts.send_far(OWN_B)
    next_sum(1, "y")
    send(("sum", "yy"), sums.at[2], sums_in.at[2], text_partner)

    image_parts([(OWN, 1), (OWN, 3)])
    text_parts([(OWN, 1), (OWN, 3)])
    texts.send_near(OWN_A)
    image_ready([(OWN, 1), (OWN, 3)])
    images.send_near(OWN_A)
    image_parts([(PAIR, 0), (OWN, 0)])
    next_sum(2, "yy")
    share(0, "x", x, x_at, 3)
    text_parts([(PAIR, 0), (OWN, 0)])
    texts.send_y(0)
    image_ready([(PAIR, 0), (OWN, 0)])
    images.send_y(0)
    texts.send_near(OWN_B)
    images.send_near(OWN_B)
    shared(0, "x", x, 4)
    share(1, "z", z, z_at, 4)
    texts.send_home()
    images.send_home()
    shared(1, "z", z, 5)
    scalar_sums[...] = sums[5]
    images.finish(image_sum)
    texts.finish(text_sum)
    for copy in started:
        copy.wait_send()


def project_kernel(
    image_emb, text_emb, image_sum, text_sum, scalar_sums, log_scale, bias, loss, image_grad, text_grad, scale_grad, bias_grad
):
    scale = jnp.exp(jnp.full((1, 1), log_scale[0], jnp.float32))
    for emb, summed, grad in ((image_emb, image_sum, image_grad), (text_emb, text_sum, text_grad)):
        unit, norm = unit_rows(emb[...])
        value = summed[...] * scale
        grad[...] = (value - unit * jnp.sum(unit * value, axis=1, keepdims=True)) / norm
    total = jnp.sum(scalar_sums[...], axis=1, keepdims=True)
    loss[...] = total[0:1] / PAIRS
    bias_grad[...] = total[1:2]
    scale_grad[...] = scale * total[2:3]


PAIRS = 16384


def body(image_emb, text_emb, positive, log_scale, bias):
    rows, width = image_emb.shape
    images, texts = 16 * rows, 8 * rows
    low, full = jnp.bfloat16, jnp.float32
    vmem = pl.BlockSpec(memory_space=pltpu.VMEM)
    smem = pl.BlockSpec(memory_space=pltpu.SMEM)
    hbm = pl.BlockSpec(memory_space=pl.ANY)
    scalar = jax.ShapeDtypeStruct((1, 1), full)
    grad = jax.ShapeDtypeStruct((rows, width), full)
    home = [
        pltpu.VMEM((8, rows, width), full),
        pltpu.VMEM((3, 2, QUARTER, width), low), pltpu.VMEM((3, 2, QUARTER, width), low),
        pltpu.VMEM((3, 2, HALF, width), low), pltpu.VMEM((3, 2, HALF, width), low),
        pltpu.VMEM((4, HALF, width), low), pltpu.VMEM((4, HALF, width), low),
        pltpu.VMEM((HALF, width), low), pltpu.VMEM((HALF, width), low),
    ]
    log_scale, bias = log_scale.reshape(1), bias.reshape(1)
    image_sum, text_sum, scalar_sums = pl.pallas_call(
        kernel,
        out_shape=(grad, grad, jax.ShapeDtypeStruct((8, 128), full)),
        in_specs=[hbm, hbm, hbm, smem, smem],
        out_specs=(vmem,) * 3,
        scratch_shapes=[
            pltpu.VMEM((rows, width), low),
            pltpu.VMEM((rows, width), low),
            pltpu.VMEM((1, images), jnp.int32),
            pltpu.VMEM((images, width), low),
            pltpu.VMEM((texts, width), low),
            pltpu.VMEM((texts, images), low),
            pltpu.VMEM((8, rows, width), low),
            pltpu.VMEM((8, rows, width), low),
            *home,
            *home,
            pltpu.VMEM((3, 8, 128), full),
            pltpu.VMEM((6, 8, 128), full),
            pltpu.VMEM((3, 8, 128), full),
            pltpu.VMEM((2, 4, 8, 128), full),
            pltpu.SemaphoreType.DMA((len(NAMES),)),
            pltpu.SemaphoreType.DMA((len(NAMES),)),
            pltpu.SemaphoreType.DMA((3,)),
        ],
        compiler_params=pltpu.CompilerParams(collective_id=0, has_side_effects=True, vmem_limit_bytes=52 * 2**20),
    )(image_emb, text_emb, positive.reshape(1, images), log_scale, bias)
    loss, image_grad, text_grad, scale_grad, bias_grad = pl.pallas_call(
        project_kernel,
        out_shape=(scalar, grad, grad, scalar, scalar),
        in_specs=[vmem] * 5 + [smem] * 2,
        out_specs=(vmem,) * 5,
        compiler_params=pltpu.CompilerParams(vmem_limit_bytes=16 * 2**20),
    )(image_emb, text_emb, image_sum, text_sum, scalar_sums, log_scale, bias)
    return loss.reshape(()), image_grad, text_grad, scale_grad.reshape(()), bias_grad.reshape(())


def solution(mesh):
    placed = (P(("img", "txt"), None), P(("txt", "img"), None), P("img"), P(), P())
    return jax.shard_map(
        body,
        mesh=mesh,
        in_specs=placed,
        out_specs=(P(), P(("img", "txt"), None), P(("txt", "img"), None), P(), P()),
        check_vma=False,
    )
```

time: 388 us -> 68.7 us (0.18)
  waiting for transfers between devices: 172 us -> 0 us
  matrix products: 77.8 us -> 0 us
  blocking collectives: 74.4 us -> 0 us
  Pallas kernels: 0 us -> 64.6 us
  other arithmetic: 35.5 us -> 0 us
  between operations: 18.1 us -> 1.97 us
  loops' own time: 7.85 us -> 0 us
    all_gather x2 -> x0, waiting for transfers between devices: 91.7 us -> none  [the longest x1 59.1 us: body(): text_full = lax.all_gather(text_emb, 'img', axis=0, tiled=True)]
    reduce_scatter x2 -> x0, waiting for transfers between devices: 79.1 us -> none  [the longest x1 74 us: body(): lax.psum_scatter(image_partial, 'txt', scatter_dimension=0, tiled=True)]
    dot_general x12 -> x0, matrix products: 77.8 us -> none  [the longest x4 32 us: step(): lax.dot_general(weight_low, rows_low, (((0,), (0,)), ((), ())), preferred...]
    psum x1 -> x0, blocking collectives: 74.4 us -> none  [body(): lax.psum((loss_part, weight_part, cos_part), ('img', 'txt'))]
    pallas_call x0 -> x2, Pallas kernels: none -> 64.6 us  [the longest x1 63.1 us: body(): pl.pallas_call(kernel, out_shape=(grad, grad, jax.ShapeDtypeStruct((8, 12...]
    div x4 -> x0, other arithmetic: 14.1 us -> none  [the longest x2 9.66 us: unit_rows(): return (values / norm, norm)]
    mul x2 -> x0, other arithmetic: 12.9 us -> none  [the longest x1 8.02 us: body(): image_partial = scale * image_parts.reshape(image_rows, width)]
    reduce_sum x4 -> x0, other arithmetic: 8.57 us -> none  [the longest x2 5.82 us: unit_rows(): norm = jnp.sqrt(jnp.sum(values * values, axis=1, keepdims=True) + EPS)]
  transfers between devices with their start and end apart: 4 -> 0, of which waited for: 4 -> 0; matrix products, arithmetic and copies ran while one was open for 5% -> 0% of each run, Pallas kernels for 0% -> 0%
where the time goes in v2:
time: 68.7 us; the launch traced here: 68.5 us
  Pallas kernels  64.6 us (94%)
  between operations  1.97 us (3%)
  local copies, waits for them, and re-layouts  1.92 us (3%)
    pallas_call x1, Pallas kernels, body(): pl.pallas_call(kernel, out_shape=(grad, grad, jax.ShapeDtypeStruct((8, 12...  63.1 us
    unnamed x6, local copies, waits for them, and re-layouts  1.92 us
    pallas_call x1, Pallas kernels, body(): pl.pallas_call(project_kernel, out_shape=(scalar, grad, grad, scalar, sca...  1.47 us

profile of v2, /device:TPU:0, one launch (start us, length us, event | category | flops | bytes accessed | tf_op | source)
XLA Modules:
  0.0 68.5 jit_solution(9644845343673050151)
XLA Ops:
  0.6 0.0 copy-start.2
  1.9 0.0 copy-done.2
  2.0 0.0 copy-start
  2.0 1.0 %copy-done = bf16[128,1152]{1,0:T(8,128)(2,1)S(1)} copy-done((bf16[128,1152]{1,0:T(8,128)(2,1)S(1)}, bf16[128,1152]{1,0:T(8,128)(2,1)}, u32[]{:S(2)}) %copy-start) | copy-done | bytes 294936
  2.9 0.0 copy-start.1
  2.9 1.0 %copy-done.1 = bf16[128,1152]{1,0:T(8,128)(2,1)S(1)} copy-done((bf16[128,1152]{1,0:T(8,128)(2,1)S(1)}, bf16[128,1152]{1,0:T(8,128)(2,1)}, u32[]{:S(2)}) %copy-start.1) | copy-done | bytes 294936
  3.9 63.1 %shard_map.92 = (f32[128,1152]{1,0:T(8,128)S(1)}, f32[128,1152]{1,0:T(8,128)S(1)}, f32[8,128]{1,0:T(8,128)S(1)}) custom-call(bf16[128,1152]{1,0:T(8,128)(2,1)S(1)} %copy-done, bf16[128,1152]{1,0:T(8,128)(2,1)S(1)} %copy-done.1, s32[1,2048]{1,0:T(1,128)S(1)} %bitcast.10, f32[1]{0:T(128)} %bitcast.6.log_scale, f32[1]{0:T(128)} %bitcast.8.bias), custom_call_target="tpu_custom_call" | custom-call | tf_op jit(solution)/shard_map/pallas_call | solution.py:470
  67.0 1.5 %shard_map.93 = (f32[1,1]{1,0:T(1,128)}, f32[128,1152]{1,0:T(8,128)}, f32[128,1152]{1,0:T(8,128)}, f32[1,1]{1,0:T(1,128)}, f32[1,1]{1,0:T(1,128)}) custom-call(bf16[128,1152]{1,0:T(8,128)(2,1)S(1)} %copy-done, bf16[128,1152]{1,0:T(8,128)(2,1)S(1)} %copy-done.1, f32[128,1152]{1,0:T(8,128)S(1)} %get-tuple-element.13.image_sum, ...), custom_call_target="tpu_custom_call" | custom-call | tf_op jit(solution)/shard_map/pallas_call | solution.py:496
Async XLA Ops:
  0.6 1.3 %copy-start.2 = (s32[2048]{0:T(1024)S(1)}, s32[2048]{0:T(1024)}, u32[]{:S(2)}) copy-start(s32[2048]{0:T(1024)} %param.7) | copy-start | bytes 24580
  2.0 1.0 %copy-start = (bf16[128,1152]{1,0:T(8,128)(2,1)S(1)}, bf16[128,1152]{1,0:T(8,128)(2,1)}, u32[]{:S(2)}) copy-start(bf16[128,1152]{1,0:T(8,128)(2,1)} %image_emb.3) | copy-start | bytes 884740
  2.9 1.0 %copy-start.1 = (bf16[128,1152]{1,0:T(8,128)(2,1)S(1)}, bf16[128,1152]{1,0:T(8,128)(2,1)}, u32[]{:S(2)}) copy-start(bf16[128,1152]{1,0:T(8,128)(2,1)} %text_emb.3) | copy-start | bytes 884740

commit v3 on v2

--- a/solution.py
+++ b/solution.py
@@ -11,8 +11,11 @@
 OWN, PAIR = 0, 1
 ROWS = 128
 HALF = ROWS // 2
-QUARTER = ROWS // 4
 PLUS, MINUS = 0, 1
+PART = ((0, 64), (64, 64))
+SPLIT = (((0, 32), (32, 32)), ((64, 32), (96, 32)))
+HOME_PART = ((0, 80), (80, 48))
+HOME_SPLIT = (((0, 48), (48, 32)), ((80, 16), (96, 32)))
 OWN_A, OWN_B, PAIR_A = 0, 1, 2
 FIRST = [(OWN, 0), (PAIR, 0), (OWN, 1), (OWN, 3)]
 SECOND = [(PAIR, 1), (PAIR, 3), (OWN, 2)]
@@ -30,7 +33,7 @@
     NAMES += [(_kind, "home")]
 NAMES += [("core", t, d) for t in (OWN, PAIR) for d in range(4)]
 NAMES += [("coresum", t, d) for t in (OWN, PAIR) for d in range(4)]
-NAMES += [("sum", stage) for stage in ("core", "y", "yy")]
+NAMES += [("sum", "y", d) for d in range(1, 8)]
 NAMES += [("sum", axis, d) for axis in ("x", "z") for d in (1, 2, 3)]
 IDS = {name: i for i, name in enumerate(NAMES)}
 
@@ -39,6 +42,9 @@
     values = emb.astype(jnp.float32)
     norm = jnp.sqrt(jnp.sum(values * values, axis=1, keepdims=True) + EPS)
     return values / norm, norm
+
+
+PAIRS = 16384
 
 
 class Ring:
@@ -48,7 +54,7 @@
         self.slot = slot
 
     def part(self, t, d, first, count):
-        return self.rows.at[pl.ds(pl.multiple_of(self.slot(t, d) * ROWS + first, QUARTER), count)]
+        return self.rows.at[pl.ds(pl.multiple_of(self.slot(t, d) * ROWS + first, 16), count)]
 
 
 class Home:
@@ -63,7 +69,7 @@
     image_in, text_in, positive, image_rows, text_rows, weight_t, core_out, core_in, *rest,
 ):
     image_home, text_home = Home(*rest[:9]), Home(*rest[9:18])
-    totals, sums, sums_in, ring_sums, send_sem, recv_sem, load_sem = rest[18:]
+    totals, sums, shares, send_sem, recv_sem, load_sem = rest[18:]
     img, txt = lax.axis_index("img"), lax.axis_index("txt")
     z, yh = lax.div(img, 2), lax.rem(img, 2)
     yl, x, c = lax.div(txt, 8), lax.rem(lax.div(txt, 2), 4), lax.rem(txt, 2)
@@ -91,7 +97,9 @@
     z_at = {d: device(z=step(z, d)) for d in (1, 2, 3)}
 
     barrier = pltpu.get_barrier_semaphore()
-    partners = [sibling, image_partner, text_partner, *x_at.values(), *z_at.values()]
+    y_at = {a * 4 + b * 2 + e: device(yh=other(yh, a), yl=other(yl, b), c=other(c, e)) for a in (0, 1) for b in (0, 1) for e in (0, 1)}
+    del y_at[0]
+    partners = [*y_at.values(), *x_at.values(), *z_at.values()]
     for partner in partners:
         pl.semaphore_signal(barrier, inc=1, device_id=partner, device_id_type=MESH)
 
@@ -148,53 +156,50 @@
         for t, d in blocks:
             recv(("core", t, d), image_rows.at[block(image_slot(t, d, 1 - c))])
 
-    def quarter(way, h):
-        return h * HALF + way * QUARTER, QUARTER
-
     def near(way):
         return 3 if way == PLUS else 1
 
     def gather_start(ring):
-        forward(ring, ("y", 0), OWN, 0, 0, HALF, ring.partner)
+        forward(ring, ("y", 0), OWN, 0, *PART[0], ring.partner)
         for h in (1, 0):
             for way in (PLUS, MINUS):
-                forward(ring, ("own", way, h), OWN, 0, h * HALF, HALF, ring.to[way])
-        forward(ring, ("y", 1), OWN, 0, HALF, HALF, ring.partner)
+                forward(ring, ("own", way, h), OWN, 0, *PART[h], ring.to[way])
+        forward(ring, ("y", 1), OWN, 0, *PART[1], ring.partner)
 
     def gather_ring(ring, h):
         for way in (PLUS, MINUS):
             d = near(way)
-            arrived(ring, ("own", way, h), OWN, d, h * HALF, HALF)
-            forward(ring, ("own2", way, h), OWN, d, *quarter(way, h), ring.to[way])
+            arrived(ring, ("own", way, h), OWN, d, *PART[h])
+            forward(ring, ("own2", way, h), OWN, d, *SPLIT[h][way], ring.to[way])
             if h == 1:
-                forward(ring, ("y_ring", d), OWN, d, HALF, HALF, ring.partner)
+                forward(ring, ("y_ring", d), OWN, d, *PART[1], ring.partner)
 
     def gather_pair(ring):
-        arrived(ring, ("y", 0), PAIR, 0, 0, HALF)
+        arrived(ring, ("y", 0), PAIR, 0, *PART[0])
         for way in (PLUS, MINUS):
-            forward(ring, ("pair", way), PAIR, 0, 0, HALF, ring.to[way])
+            forward(ring, ("pair", way), PAIR, 0, *PART[0], ring.to[way])
 
     def gather_far(ring):
         for way in (PLUS, MINUS):
-            arrived(ring, ("own2", way, 1), OWN, 2, *quarter(way, 1))
-        forward(ring, ("y_ring", 2), OWN, 2, HALF, HALF, ring.partner)
+            arrived(ring, ("own2", way, 1), OWN, 2, *SPLIT[1][way])
+        forward(ring, ("y_ring", 2), OWN, 2, *PART[1], ring.partner)
 
     def gather_pair_ring(ring):
         for way in (PLUS, MINUS):
             d = near(way)
-            arrived(ring, ("pair", way), PAIR, d, 0, HALF)
-            forward(ring, ("pair2", way), PAIR, d, *quarter(way, 0), ring.to[way])
+            arrived(ring, ("pair", way), PAIR, d, *PART[0])
+            forward(ring, ("pair2", way), PAIR, d, *SPLIT[0][way], ring.to[way])
 
     def gather_second(ring):
         for d in (1, 3):
-            arrived(ring, ("y_ring", d), PAIR, d, HALF, HALF)
+            arrived(ring, ("y_ring", d), PAIR, d, *PART[1])
         for way in (PLUS, MINUS):
-            arrived(ring, ("own2", way, 0), OWN, 2, *quarter(way, 0))
+            arrived(ring, ("own2", way, 0), OWN, 2, *SPLIT[0][way])
 
     def gather_last(ring):
-        arrived(ring, ("y_ring", 2), PAIR, 2, HALF, HALF)
+        arrived(ring, ("y_ring", 2), PAIR, 2, *PART[1])
         for way in (PLUS, MINUS):
-            arrived(ring, ("pair2", way), PAIR, 2, *quarter(way, 0))
+            arrived(ring, ("pair2", way), PAIR, 2, *SPLIT[0][way])
 
     scale = jnp.exp(jnp.full((1, 256), log_scale[0], jnp.float32))
     scale2 = scale * LOG2E
@@ -262,22 +267,24 @@
         for t, d in blocks:
             recv(("coresum", t, d), core_in.at[place(t, d)])
 
-    def image_part(t, d, half):
-        rows = slice(half * HALF, (half + 1) * HALF)
-        return image_home.own[place(t, d), rows] + core_in[place(t, d), rows].astype(jnp.float32)
-
-    def text_part(t, d, half):
-        return text_home.own[place(t, d), half * HALF : (half + 1) * HALF]
+    def rows_of(h):
+        return slice(HOME_PART[h][0], sum(HOME_PART[h]))
+
+    def image_part(t, d, h):
+        return image_home.own[place(t, d), rows_of(h)] + core_in[place(t, d), rows_of(h)].astype(jnp.float32)
+
+    def text_part(t, d, h):
+        return text_home.own[place(t, d), rows_of(h)]
 
     class Sums:
         def __init__(self, ring, home, part):
             self.ring, self.home, self.part = ring, home, part
 
-        def send(self, name, src, dst, to):
-            send((self.ring.kind, *name), src, dst, to)
-
-        def recv(self, name, dst):
-            recv((self.ring.kind, *name), dst)
+        def send(self, name, out, into, to):
+            send((self.ring.kind, *name), out, into, to)
+
+        def recv(self, name, into):
+            recv((self.ring.kind, *name), into)
 
         def value(self, part, d):
             if part == OWN_B:
@@ -289,30 +296,39 @@
             self.home.y_out[d] = self.part(PAIR, d, 1).astype(jnp.bfloat16)
             self.send(("y_sum", d), self.home.y_out.at[d], self.home.y_in.at[d], self.ring.partner)
 
+        def split(self, part, way):
+            h = 1 if part == OWN_B else 0
+            first, count = HOME_SPLIT[h][way]
+            return first - HOME_PART[h][0], count
+
         def send_far(self, part):
             value = self.value(part, 2).astype(jnp.bfloat16)
             for way in (PLUS, MINUS):
-                self.home.far_out[part, way] = value[way * QUARTER : (way + 1) * QUARTER]
-                out, into = self.home.far_out.at[part, way], self.home.far_in.at[part, way]
+                first, count = self.split(part, way)
+                self.home.far_out[part, way, :count] = value[first : first + count]
+                out, into = self.home.far_out.at[part, way, pl.ds(0, count)], self.home.far_in.at[part, way, pl.ds(0, count)]
                 self.send(("far", way, part), out, into, self.ring.to[way])
 
         def send_near(self, part):
             for way in (PLUS, MINUS):
                 value = self.value(part, 1 if way == PLUS else 3)
-                self.recv(("far", way, part), self.home.far_in.at[part, way])
-                mine = slice(way * QUARTER, (way + 1) * QUARTER)
-                rest = slice((1 - way) * QUARTER, (2 - way) * QUARTER)
-                more = self.home.far_in[part, way].astype(jnp.float32)
-                self.home.near_out[part, way, mine] = (value[mine] + more).astype(jnp.bfloat16)
-                self.home.near_out[part, way, rest] = value[rest].astype(jnp.bfloat16)
-                out, into = self.home.near_out.at[part, way], self.home.near_in.at[part, way]
+                rows = value.shape[0]
+                first, count = self.split(part, way)
+                out, into = self.home.near_out.at[part, way, pl.ds(0, rows)], self.home.near_in.at[part, way, pl.ds(0, rows)]
+                self.recv(("far", way, part), self.home.far_in.at[part, way, pl.ds(0, count)])
+                more = self.home.far_in[part, way, :count].astype(jnp.float32)
+                for lo, hi in ((0, first), (first, first + count), (first + count, rows)):
+                    if lo < hi:
+                        piece = value[lo:hi] + more if lo == first else value[lo:hi]
+                        self.home.near_out[part, way, lo:hi] = piece.astype(jnp.bfloat16)
                 self.send(("near", way, part), out, into, self.ring.to[way])
 
         def ring_sum(self, part):
             value = self.value(part, 0)
+            rows = value.shape[0]
             for way in (PLUS, MINUS):
-                self.recv(("near", way, part), self.home.near_in.at[part, way])
-                value = value + self.home.near_in[part, way].astype(jnp.float32)
+                self.recv(("near", way, part), self.home.near_in.at[part, way, pl.ds(0, rows)])
+                value = value + self.home.near_in[part, way, :rows].astype(jnp.float32)
             return value
 
         def send_home(self):
@@ -320,26 +336,33 @@
             self.send(("home",), self.home.home_out, self.home.home_in, self.ring.partner)
 
         def finish(self, out):
-            out[HALF:] = self.ring_sum(OWN_B)
+            out[rows_of(1)] = self.ring_sum(OWN_B)
             value = self.ring_sum(OWN_A)
             self.recv(("home",), self.home.home_in)
-            out[:HALF] = value + self.home.home_in[...].astype(jnp.float32)
+            out[rows_of(0)] = value + self.home.home_in[...].astype(jnp.float32)
 
     images, texts = Sums(image, image_home, image_part), Sums(text, text_home, text_part)
 
-    def next_sum(i, name):
-        recv(("sum", name), sums_in.at[i])
-        sums[i + 1] = sums[i] + sums_in[i]
-
-    def share(i, axis, me, at, source):
-        ring_sums[i, me] = sums[source]
-        for d in (1, 2, 3):
-            send(("sum", axis, d), sums.at[source], ring_sums.at[i, me], at[d])
-
-    def shared(i, axis, me, into):
-        for d in (1, 2, 3):
-            recv(("sum", axis, d), ring_sums.at[i, step(me, 4 - d)])
-        sums[into] = (ring_sums[i, 0] + ring_sums[i, 1]) + (ring_sums[i, 2] + ring_sums[i, 3])
+    def slot_y(d):
+        return other(yh, d // 4) * 4 + other(yl, d // 2 % 2) * 2 + other(c, d % 2)
+
+    stages = {
+        "y": (0, 8, slot_y, y_at),
+        "x": (1, 4, lambda d: step(x, (4 - d) % 4), x_at),
+        "z": (2, 4, lambda d: step(z, (4 - d) % 4), z_at),
+    }
+
+    def share(axis):
+        i, _, slot, peers = stages[axis]
+        shares[i, slot(0)] = sums[i]
+        for d, peer in peers.items():
+            send(("sum", axis, d), sums.at[i], shares.at[i, slot(0)], peer)
+
+    def shared(axis):
+        i, count, slot, peers = stages[axis]
+        for d in peers:
+            recv(("sum", axis, d), shares.at[i, slot(d)])
+        sums[i + 1] = sum(shares[i, k] for k in range(count))
 
     gather_start(image)
     gather_start(text)
@@ -351,7 +374,7 @@
     for ring in (image, text):
         gather_ring(ring, 0)
     for ring in (image, text):
-        arrived(ring, ("y", 1), PAIR, 0, HALF, HALF)
+        arrived(ring, ("y", 1), PAIR, 0, *PART[1])
     to_sibling(FIRST[1:])
     gather_far(image)
     gather_far(text)
@@ -369,31 +392,26 @@
     every = FIRST + SECOND + LAST
     from_sibling(SECOND)
     tile(every, OWN, 2)
-    image_parts([(OWN, 2)])
-    tiles(LAST, 2, lambda i: (i, 0))
-    tiles(LAST, 2, lambda i: (OWN, 1 + 2 * i))
     from_sibling(LAST)
     tile(every, PAIR, 2)
-    image_parts([(PAIR, 2)])
-    image_ready([(OWN, 2)])
-    images.send_far(OWN_A)
+    image_parts([(PAIR, 2), (OWN, 2)])
     tiles(every, 2, lambda i: (PAIR, 1 + 2 * i))
-    image_ready([(PAIR, 2)])
+    image_ready([(PAIR, 2), (OWN, 2)])
     images.send_y(2)
     images.send_far(PAIR_A)
-
+    images.send_far(OWN_A)
+    tiles(LAST, 4, first_place)
     for i in range(3):
         sums[0, i : i + 1] = jnp.sum(totals[i], axis=0, keepdims=True)
     sums[0, 3:] = jnp.zeros((5, 128), jnp.float32)
-    send(("sum", "core"), sums.at[0], sums_in.at[0], sibling)
-
+    share("y")
     text_parts([(PAIR, 2), (OWN, 2)])
     texts.send_y(2)
     texts.send_far(PAIR_A)
     texts.send_far(OWN_A)
     image_parts([(PAIR, 1), (PAIR, 3)])
-    next_sum(0, "core")
-    send(("sum", "y"), sums.at[1], sums_in.at[1], image_partner)
+    shared("y")
+    share("x")
     text_parts([(PAIR, 1), (PAIR, 3)])
     texts.send_y(1)
     texts.send_y(3)
@@ -403,30 +421,28 @@
     images.send_near(PAIR_A)
     texts.send_near(PAIR_A)
     images.send_far(OWN_B)
+    image_parts([(OWN, 1), (OWN, 3)])
+    shared("x")
+    share("z")
     texts.send_far(OWN_B)
-    next_sum(1, "y")
-    send(("sum", "yy"), sums.at[2], sums_in.at[2], text_partner)
-
-    image_parts([(OWN, 1), (OWN, 3)])
+    image_parts([(PAIR, 0)])
+    text_parts([(PAIR, 0)])
+    texts.send_y(0)
     text_parts([(OWN, 1), (OWN, 3)])
-    texts.send_near(OWN_A)
     image_ready([(OWN, 1), (OWN, 3)])
     images.send_near(OWN_A)
-    image_parts([(PAIR, 0), (OWN, 0)])
-    next_sum(2, "yy")
-    share(0, "x", x, x_at, 3)
-    text_parts([(PAIR, 0), (OWN, 0)])
-    texts.send_y(0)
-    image_ready([(PAIR, 0), (OWN, 0)])
+    texts.send_near(OWN_A)
+    image_ready([(PAIR, 0)])
     images.send_y(0)
+    images.send_home()
+    texts.send_home()
+    images.send_near(OWN_B)
     texts.send_near(OWN_B)
-    images.send_near(OWN_B)
-    shared(0, "x", x, 4)
-    share(1, "z", z, z_at, 4)
-    texts.send_home()
-    images.send_home()
-    shared(1, "z", z, 5)
-    scalar_sums[...] = sums[5]
+    image_parts([(OWN, 0)])
+    text_parts([(OWN, 0)])
+    shared("z")
+    scalar_sums[...] = sums[3]
+    image_ready([(OWN, 0)])
     images.finish(image_sum)
     texts.finish(text_sum)
     for copy in started:
@@ -447,9 +463,6 @@
     scale_grad[...] = scale * total[2:3]
 
 
-PAIRS = 16384
-
-
 def body(image_emb, text_emb, positive, log_scale, bias):
     rows, width = image_emb.shape
     images, texts = 16 * rows, 8 * rows
@@ -461,10 +474,10 @@
     grad = jax.ShapeDtypeStruct((rows, width), full)
     home = [
         pltpu.VMEM((8, rows, width), full),
-        pltpu.VMEM((3, 2, QUARTER, width), low), pltpu.VMEM((3, 2, QUARTER, width), low),
-        pltpu.VMEM((3, 2, HALF, width), low), pltpu.VMEM((3, 2, HALF, width), low),
-        pltpu.VMEM((4, HALF, width), low), pltpu.VMEM((4, HALF, width), low),
-        pltpu.VMEM((HALF, width), low), pltpu.VMEM((HALF, width), low),
+        pltpu.VMEM((3, 2, 48, width), low), pltpu.VMEM((3, 2, 48, width), low),
+        pltpu.VMEM((3, 2, 80, width), low), pltpu.VMEM((3, 2, 80, width), low),
+        pltpu.VMEM((4, 48, width), low), pltpu.VMEM((4, 48, width), low),
+        pltpu.VMEM((80, width), low), pltpu.VMEM((80, width), low),
     ]
     log_scale, bias = log_scale.reshape(1), bias.reshape(1)
     image_sum, text_sum, scalar_sums = pl.pallas_call(
@@ -484,15 +497,14 @@
             *home,
             *home,
             pltpu.VMEM((3, 8, 128), full),
-            pltpu.VMEM((6, 8, 128), full),
-            pltpu.VMEM((3, 8, 128), full),
-            pltpu.VMEM((2, 4, 8, 128), full),
+            pltpu.VMEM((4, 8, 128), full),
+            pltpu.VMEM((3, 8, 8, 128), full),
             pltpu.SemaphoreType.DMA((len(NAMES),)),
             pltpu.SemaphoreType.DMA((len(NAMES),)),
             pltpu.SemaphoreType.DMA((3,)),
         ],
         compiler_params=pltpu.CompilerParams(collective_id=0, has_side_effects=True, vmem_limit_bytes=52 * 2**20),
-    )(image_emb, text_emb, positive.reshape(1, images), log_scale, bias)
+    )(*(pltpu.with_memory_space_constraint(a, pltpu.HBM) for a in (image_emb, text_emb, positive.reshape(1, images))), log_scale, bias)
     loss, image_grad, text_grad, scale_grad, bias_grad = pl.pallas_call(
         project_kernel,
         out_shape=(scalar, grad, grad, scalar, scalar),

time: 68.7 us -> 62.2 us (0.905)
  Pallas kernels: 64.6 us -> 60.1 us
  local copies, waits for them, and re-layouts: 1.92 us -> 0.01 us
    pallas_call x1, Pallas kernels: 63.1 us -> 58.6 us  [body(): pl.pallas_call(kernel, out_shape=(grad, grad, jax.ShapeDtypeStruct((8, 12...]
    unnamed x6 -> x4, local copies, waits for them, and re-layouts: 1.92 us -> 0.01 us
where the time goes in v3:
time: 62.2 us; the launch traced here: 62 us
  Pallas kernels  60.1 us (97%)
  between operations  1.96 us (3%)
    pallas_call x1, Pallas kernels, body(): pl.pallas_call(kernel, out_shape=(grad, grad, jax.ShapeDtypeStruct((8, 12...  58.6 us
    pallas_call x1, Pallas kernels, body(): pl.pallas_call(project_kernel, out_shape=(scalar, grad, grad, scalar, sca...  1.43 us

profile of v3, /device:TPU:0, one launch (start us, length us, event | category | flops | bytes accessed | tf_op | source)
XLA Modules:
  0.0 62.0 jit_solution(9871879024964029991)
XLA Ops:
  1.9 0.0 copy-start
  1.9 0.0 copy-start.1
  1.9 58.6 %shard_map.92 = (f32[128,1152]{1,0:T(8,128)S(1)}, f32[128,1152]{1,0:T(8,128)S(1)}, f32[8,128]{1,0:T(8,128)S(1)}) custom-call(bf16[128,1152]{1,0:T(8,128)(2,1)} %image_emb.3, bf16[128,1152]{1,0:T(8,128)(2,1)} %text_emb.3, s32[1,2048]{1,0:T(1,128)} %bitcast.10, f32[1]{0:T(128)} %bitcast.6.log_scale, f32[1]{0:T(128)} %bitcast.8.bias), custom_call_target="tpu_custom_call" | custom-call | tf_op jit(solution)/shard_map/pallas_call | solution.py:483
  60.6 0.0 copy-done
  60.6 0.0 copy-done.1
  60.6 1.4 %shard_map.93 = (f32[1,1]{1,0:T(1,128)}, f32[128,1152]{1,0:T(8,128)}, f32[128,1152]{1,0:T(8,128)}, f32[1,1]{1,0:T(1,128)}, f32[1,1]{1,0:T(1,128)}) custom-call(bf16[128,1152]{1,0:T(8,128)(2,1)S(1)} %copy-done, bf16[128,1152]{1,0:T(8,128)(2,1)S(1)} %copy-done.1, f32[128,1152]{1,0:T(8,128)S(1)} %get-tuple-element.13.image_sum, ...), custom_call_target="tpu_custom_call" | custom-call | tf_op jit(solution)/shard_map/pallas_call | solution.py:508
Async XLA Ops:
  1.9 58.7 %copy-start = (bf16[128,1152]{1,0:T(8,128)(2,1)S(1)}, bf16[128,1152]{1,0:T(8,128)(2,1)}, u32[]{:S(2)}) copy-start(bf16[128,1152]{1,0:T(8,128)(2,1)} %image_emb.3) | copy-start | bytes 884740
  1.9 58.7 %copy-start.1 = (bf16[128,1152]{1,0:T(8,128)(2,1)S(1)}, bf16[128,1152]{1,0:T(8,128)(2,1)}, u32[]{:S(2)}) copy-start(bf16[128,1152]{1,0:T(8,128)(2,1)} %text_emb.3) | copy-start | bytes 884740

commit v4 on v3

--- a/solution.py
+++ b/solution.py
@@ -379,9 +379,10 @@
     gather_far(image)
     gather_far(text)
     from_sibling(FIRST)
-    tiles(FIRST, 4, first_place)
+    tiles(FIRST, 2, lambda i: (i, 0))
+    gather_pair_ring(text)
     gather_pair_ring(image)
-    gather_pair_ring(text)
+    tiles(FIRST, 2, lambda i: (OWN, 1 + 2 * i))
     gather_second(image)
     to_sibling(SECOND)
     gather_second(text)
@@ -390,6 +391,7 @@
     to_sibling(LAST)
     gather_last(text)
     every = FIRST + SECOND + LAST
+    gathered = len(started)
     from_sibling(SECOND)
     tile(every, OWN, 2)
     from_sibling(LAST)
@@ -438,15 +440,17 @@
     texts.send_home()
     images.send_near(OWN_B)
     texts.send_near(OWN_B)
+    for copy in started[:gathered]:
+        copy.wait_send()
     image_parts([(OWN, 0)])
     text_parts([(OWN, 0)])
+    for copy in started[gathered:]:
+        copy.wait_send()
     shared("z")
     scalar_sums[...] = sums[3]
     image_ready([(OWN, 0)])
     images.finish(image_sum)
     texts.finish(text_sum)
-    for copy in started:
-        copy.wait_send()
 
 
 def project_kernel(

time: 62.2 us -> 61.2 us (0.984)
  Pallas kernels: 60.1 us -> 59 us
    pallas_call x1, Pallas kernels: 58.6 us -> 57.6 us  [body(): pl.pallas_call(kernel, out_shape=(grad, grad, jax.ShapeDtypeStruct((8, 12...]
where the time goes in v4:
time: 61.2 us; the launch traced here: 61 us
  Pallas kernels  59 us (96%)
  between operations  1.96 us (3%)
    pallas_call x1, Pallas kernels, body(): pl.pallas_call(kernel, out_shape=(grad, grad, jax.ShapeDtypeStruct((8, 12...  57.6 us
    pallas_call x1, Pallas kernels, body(): pl.pallas_call(project_kernel, out_shape=(scalar, grad, grad, scalar, sca...  1.43 us

profile of v4, /device:TPU:0, one launch (start us, length us, event | category | flops | bytes accessed | tf_op | source)
XLA Modules:
  0.0 61.0 jit_solution(13381440817999573831)
XLA Ops:
  1.9 0.0 copy-start
  1.9 0.0 copy-start.1
  1.9 57.6 %shard_map.92 = (f32[128,1152]{1,0:T(8,128)S(1)}, f32[128,1152]{1,0:T(8,128)S(1)}, f32[8,128]{1,0:T(8,128)S(1)}) custom-call(bf16[128,1152]{1,0:T(8,128)(2,1)} %image_emb.3, bf16[128,1152]{1,0:T(8,128)(2,1)} %text_emb.3, s32[1,2048]{1,0:T(1,128)} %bitcast.10, f32[1]{0:T(128)} %bitcast.6.log_scale, f32[1]{0:T(128)} %bitcast.8.bias), custom_call_target="tpu_custom_call" | custom-call | tf_op jit(solution)/shard_map/pallas_call | solution.py:487
  59.6 0.0 copy-done
  59.6 0.0 copy-done.1
  59.6 1.4 %shard_map.93 = (f32[1,1]{1,0:T(1,128)}, f32[128,1152]{1,0:T(8,128)}, f32[128,1152]{1,0:T(8,128)}, f32[1,1]{1,0:T(1,128)}, f32[1,1]{1,0:T(1,128)}) custom-call(bf16[128,1152]{1,0:T(8,128)(2,1)S(1)} %copy-done, bf16[128,1152]{1,0:T(8,128)(2,1)S(1)} %copy-done.1, f32[128,1152]{1,0:T(8,128)S(1)} %get-tuple-element.13.image_sum, ...), custom_call_target="tpu_custom_call" | custom-call | tf_op jit(solution)/shard_map/pallas_call | solution.py:512
Async XLA Ops:
  1.9 57.7 %copy-start = (bf16[128,1152]{1,0:T(8,128)(2,1)S(1)}, bf16[128,1152]{1,0:T(8,128)(2,1)}, u32[]{:S(2)}) copy-start(bf16[128,1152]{1,0:T(8,128)(2,1)} %image_emb.3) | copy-start | bytes 884740
  1.9 57.7 %copy-start.1 = (bf16[128,1152]{1,0:T(8,128)(2,1)S(1)}, bf16[128,1152]{1,0:T(8,128)(2,1)}, u32[]{:S(2)}) copy-start(bf16[128,1152]{1,0:T(8,128)(2,1)} %text_emb.3) | copy-start | bytes 884740

commit v5 on v4

--- a/solution.py
+++ b/solution.py
@@ -229,7 +229,7 @@
                 product = e8[0]
                 for k in range(1, 8):
                     product = product * u8[k] + e8[k]
-                add[0] += jnp.log1p(product)
+                add[0] += jnp.log(1.0 + product)
                 add[1] += jnp.sum(w.reshape(8, 8, 256), axis=0)
                 add[2] += jnp.sum((w * cos).reshape(8, 8, 256), axis=0)
         for i in range(3):
@@ -378,10 +378,11 @@
     to_sibling(FIRST[1:])
     gather_far(image)
     gather_far(text)
-    from_sibling(FIRST)
+    from_sibling(FIRST[:2])
     tiles(FIRST, 2, lambda i: (i, 0))
     gather_pair_ring(text)
     gather_pair_ring(image)
+    from_sibling(FIRST[2:])
     tiles(FIRST, 2, lambda i: (OWN, 1 + 2 * i))
     gather_second(image)
     to_sibling(SECOND)

time: 61.2 us -> 61.1 us (level)
  no operation moved by 1% of the time
where the time goes in v5:
time: 61.1 us; the launch traced here: 60.9 us
  Pallas kernels  59 us (97%)
  between operations  1.96 us (3%)
    pallas_call x1, Pallas kernels, body(): pl.pallas_call(kernel, out_shape=(grad, grad, jax.ShapeDtypeStruct((8, 12...  57.5 us
    pallas_call x1, Pallas kernels, body(): pl.pallas_call(project_kernel, out_shape=(scalar, grad, grad, scalar, sca...  1.43 us

profile of v5, /device:TPU:0, one launch (start us, length us, event | category | flops | bytes accessed | tf_op | source)
XLA Modules:
  0.0 60.9 jit_solution(18405621145025290859)
XLA Ops:
  1.9 0.0 copy-start
  1.9 0.0 copy-start.1
  1.9 57.5 %shard_map.92 = (f32[128,1152]{1,0:T(8,128)S(1)}, f32[128,1152]{1,0:T(8,128)S(1)}, f32[8,128]{1,0:T(8,128)S(1)}) custom-call(bf16[128,1152]{1,0:T(8,128)(2,1)} %image_emb.3, bf16[128,1152]{1,0:T(8,128)(2,1)} %text_emb.3, s32[1,2048]{1,0:T(1,128)} %bitcast.10, f32[1]{0:T(128)} %bitcast.6.log_scale, f32[1]{0:T(128)} %bitcast.8.bias), custom_call_target="tpu_custom_call" | custom-call | tf_op jit(solution)/shard_map/pallas_call | solution.py:488
  59.5 0.0 copy-done
  59.5 0.0 copy-done.1
  59.5 1.4 %shard_map.93 = (f32[1,1]{1,0:T(1,128)}, f32[128,1152]{1,0:T(8,128)}, f32[128,1152]{1,0:T(8,128)}, f32[1,1]{1,0:T(1,128)}, f32[1,1]{1,0:T(1,128)}) custom-call(bf16[128,1152]{1,0:T(8,128)(2,1)S(1)} %copy-done, bf16[128,1152]{1,0:T(8,128)(2,1)S(1)} %copy-done.1, f32[128,1152]{1,0:T(8,128)S(1)} %get-tuple-element.13.image_sum, ...), custom_call_target="tpu_custom_call" | custom-call | tf_op jit(solution)/shard_map/pallas_call | solution.py:513
Async XLA Ops:
  1.9 57.6 %copy-start = (bf16[128,1152]{1,0:T(8,128)(2,1)S(1)}, bf16[128,1152]{1,0:T(8,128)(2,1)}, u32[]{:S(2)}) copy-start(bf16[128,1152]{1,0:T(8,128)(2,1)} %image_emb.3) | copy-start | bytes 884740
  1.9 57.6 %copy-start.1 = (bf16[128,1152]{1,0:T(8,128)(2,1)S(1)}, bf16[128,1152]{1,0:T(8,128)(2,1)}, u32[]{:S(2)}) copy-start(bf16[128,1152]{1,0:T(8,128)(2,1)} %text_emb.3) | copy-start | bytes 884740

commit v6 on v5

--- a/solution.py
+++ b/solution.py
@@ -403,7 +403,8 @@
     images.send_y(2)
     images.send_far(PAIR_A)
     images.send_far(OWN_A)
-    tiles(LAST, 4, first_place)
+    for t, d in FIRST:
+        tile(LAST, t, d)
     for i in range(3):
         sums[0, i : i + 1] = jnp.sum(totals[i], axis=0, keepdims=True)
     sums[0, 3:] = jnp.zeros((5, 128), jnp.float32)

time: 61.1 us -> 60.9 us (level)
  no operation moved by 1% of the time
where the time goes in v6:
time: 60.9 us; the launch traced here: 60.4 us
  Pallas kernels  58.5 us (96%)
  between operations  1.96 us (3%)
    pallas_call x1, Pallas kernels, body(): pl.pallas_call(kernel, out_shape=(grad, grad, jax.ShapeDtypeStruct((8, 12...  57 us
    pallas_call x1, Pallas kernels, body(): pl.pallas_call(project_kernel, out_shape=(scalar, grad, grad, scalar, sca...  1.43 us

profile of v6, /device:TPU:0, one launch (start us, length us, event | category | flops | bytes accessed | tf_op | source)
XLA Modules:
  0.0 60.4 jit_solution(14214627391355505514)
XLA Ops:
  1.9 0.0 copy-start
  1.9 0.0 copy-start.1
  1.9 57.0 %shard_map.92 = (f32[128,1152]{1,0:T(8,128)S(1)}, f32[128,1152]{1,0:T(8,128)S(1)}, f32[8,128]{1,0:T(8,128)S(1)}) custom-call(bf16[128,1152]{1,0:T(8,128)(2,1)} %image_emb.3, bf16[128,1152]{1,0:T(8,128)(2,1)} %text_emb.3, s32[1,2048]{1,0:T(1,128)} %bitcast.10, f32[1]{0:T(128)} %bitcast.6.log_scale, f32[1]{0:T(128)} %bitcast.8.bias), custom_call_target="tpu_custom_call" | custom-call | tf_op jit(solution)/shard_map/pallas_call | solution.py:489
  59.0 0.0 copy-done
  59.0 0.0 copy-done.1
  59.0 1.4 %shard_map.93 = (f32[1,1]{1,0:T(1,128)}, f32[128,1152]{1,0:T(8,128)}, f32[128,1152]{1,0:T(8,128)}, f32[1,1]{1,0:T(1,128)}, f32[1,1]{1,0:T(1,128)}) custom-call(bf16[128,1152]{1,0:T(8,128)(2,1)S(1)} %copy-done, bf16[128,1152]{1,0:T(8,128)(2,1)S(1)} %copy-done.1, f32[128,1152]{1,0:T(8,128)S(1)} %get-tuple-element.13.image_sum, ...), custom_call_target="tpu_custom_call" | custom-call | tf_op jit(solution)/shard_map/pallas_call | solution.py:514
Async XLA Ops:
  1.9 57.1 %copy-start = (bf16[128,1152]{1,0:T(8,128)(2,1)S(1)}, bf16[128,1152]{1,0:T(8,128)(2,1)}, u32[]{:S(2)}) copy-start(bf16[128,1152]{1,0:T(8,128)(2,1)} %image_emb.3) | copy-start | bytes 884740
  1.9 57.1 %copy-start.1 = (bf16[128,1152]{1,0:T(8,128)(2,1)S(1)}, bf16[128,1152]{1,0:T(8,128)(2,1)}, u32[]{:S(2)}) copy-start(bf16[128,1152]{1,0:T(8,128)(2,1)} %text_emb.3) | copy-start | bytes 884740
